TPU v7x, 32 devices: a whole 2x2x4 slice. The times are simulated.
32 devices in a mesh: sec: 2 (over y), row: 4 (over x, core), col: 4 (over z).
Axes of the slice: x: 2, y: 2, z: 4, core: 2. Of those that a mesh axis runs over, the one named last changes fastest.
Arguments:
- sketch: float32 [32, 64, 2048], P(None, ('sec', 'row'), 'col'), parts along dimension 1, may hold values from -6 to 6
- weights: float32 [8, 64, 2048], P(None, ('sec', 'row'), 'col'), parts along dimension 1, may hold values from 0.05 to 1
Outputs:
- basis: float32 [32, 64, 2048], P(None, ('sec', 'row'), 'col'), parts along dimension 1
- factor: float32 [64, 32], P('sec'), parts along dimension 0
There are 2 independent parts, one for each index of `sec`. A program takes and returns all parts, laid end to end along the dimension named above; each array names one. Nothing has to cross between parts.
All inputs are finite; a program needn't handle non-finite values.
Results may differ from a plain program's by a relative error of at most 0.0001.
Values sent between devices are 32-bit elements; how exact they have to be, the bound alone decides.
A program may use at most 64 MiB of HBM per device.

v0:
```python
import functools

import jax
import jax.numpy as jnp
from jax import lax
from jax.experimental import pallas as pl
from jax.experimental.pallas import tpu as pltpu
from jax.sharding import PartitionSpec as P

LANES = 128
SUB = 8
NEIGHBOURS = ((-1, -1), (-1, 0), (-1, 1), (0, -1), (0, 1), (1, -1), (1, 0), (1, 1))
MESH = pl.DeviceIdType.MESH
NT = (((1,), (1,)), ((), ()))
HIGHEST = lax.Precision.HIGHEST


def split(x):
    hi = x.astype(jnp.bfloat16)
    lo = (x - hi.astype(jnp.float32)).astype(jnp.bfloat16)
    return hi, lo


def kernel(
    n, rows, cols, R, C, stages,
    sk_hbm, w_hbm, y2, tables,
    raw, wraw, ext, ext_l, ext_r, y1, y1_l, y1_r, pack, nb, held, sent,
    load_sem, row_send, row_recv, nb_send, nb_recv, gather_send, gather_recv,
):
    groups = n // SUB
    all_groups = groups + 1
    wide = cols + LANES
    i = lax.axis_index("row")
    j = lax.axis_index("col")
    has_up, has_down = i > 0, i < R - 1
    has_left, has_right = j > 0, j < C - 1

    tiles = cols // LANES
    loads = []
    for t in range(tiles):
        across = pl.ds(t * LANES, LANES)
        loads.append(pltpu.make_async_copy(sk_hbm.at[:, across], raw.at[t], load_sem.at[0, t]))
        loads.append(pltpu.make_async_copy(w_hbm.at[:, across], wraw.at[t], load_sem.at[1, t]))
    for load in loads:
        load.start()

    barrier = pltpu.get_barrier_semaphore()
    if len(stages) == 1:
        peers = [lax.rem(i * C + j + d, R * C) for d in range(1, R * C)]
        partners = [(lax.div(peer, C), lax.rem(peer, C)) for peer in peers]
    else:
        partners = [(lax.rem(i + d, R), j) for d in range(1, R)]
        partners += [(i, lax.rem(j + d, C)) for d in range(1, C)]
    for r, c in partners:
        pl.semaphore_signal(barrier, inc=1, device_id={"row": r, "col": c}, device_id_type=MESH)
    ups = ((-1, has_up), (0, None), (1, has_down))
    sides = ((-1, has_left), (1, has_right))
    for dr, ok_r in ups:
        for dc, ok_c in sides:
            if dr != 0 and len(stages) > 1:
                @pl.when(jnp.logical_and(ok_r, ok_c))
                def _(dr=dr, dc=dc):
                    pl.semaphore_signal(
                        barrier, inc=1, device_id={"row": i + dr, "col": j + dc},
                        device_id_type=MESH,
                    )
    diagonals = 0 if len(stages) == 1 else (has_up.astype(jnp.int32) + has_down.astype(jnp.int32)) * (
        has_left.astype(jnp.int32) + has_right.astype(jnp.int32)
    )

    lane = lax.broadcasted_iota(jnp.int32, (SUB, LANES), 1)

    def relayout(r):
        for t in range(tiles):
            across = slice(t * LANES, (t + 1) * LANES)
            for g in range(groups):
                ext[r + 2, g * SUB : (g + 1) * SUB, across] = raw[
                    t, pl.ds(g * SUB * rows + r, SUB, stride=rows), :
                ]
            ext[r + 2, n : n + SUB, across] = wraw[t, pl.ds(r, SUB, stride=rows), :]

    for load in loads:
        load.wait()
    for r in range(rows):
        relayout(r)

    def edge_copy(dr, dc):
        at = (1 - dr) * 2 + (0 if dc > 0 else 1)
        return pltpu.make_async_remote_copy(
            src_ref=pack, dst_ref=nb.at[at], send_sem=nb_send.at[at], recv_sem=nb_recv.at[at],
            device_id={"row": i + dr, "col": j + dc}, device_id_type=MESH,
        )

    def cond(*terms):
        terms = [t for t in terms if t is not None]
        return functools.reduce(jnp.logical_and, terms)

    def row_copy(down):
        src = rows if down else 2
        dst = 0 if down else rows + 2
        at = 0 if down else 1
        return pltpu.make_async_remote_copy(
            src_ref=ext.at[pl.ds(src, 2), :, pl.ds(0, cols)],
            dst_ref=ext.at[pl.ds(dst, 2), :, pl.ds(0, cols)],
            send_sem=row_send.at[at], recv_sem=row_recv.at[at],
            device_id={"row": i + (1 if down else -1), "col": j}, device_id_type=MESH,
        )

    pl.semaphore_wait(barrier, len(partners) + diagonals)

    @pl.when(has_down)
    def _():
        row_copy(True).start()

    @pl.when(has_up)
    def _():
        row_copy(False).start()

    packed = [jnp.zeros((SUB, LANES), jnp.float32), jnp.zeros((SUB, LANES), jnp.float32)]
    for r in range(rows):
        for g in range(all_groups):
            which, slot = (0, r * groups + g) if g < groups else (1, r)
            edge = jnp.where(
                lane < LANES // 2,
                ext[r + 2, g * SUB : (g + 1) * SUB, 0:LANES],
                ext[r + 2, g * SUB : (g + 1) * SUB, cols - LANES : cols],
            )
            moved = pltpu.roll(edge, (4 * slot + 2) % LANES, 1)
            packed[which] = jnp.where(lane // 4 == slot, moved, packed[which])
    pack[0:SUB, :] = packed[0]
    pack[SUB : 2 * SUB, :] = packed[1]

    for dr, ok_r in (ups[1], ups[0], ups[2]):
        for dc, ok_c in sides:
            @pl.when(cond(ok_r, ok_c))
            def _(dr=dr, dc=dc):
                edge_copy(dr, dc).start()

    @pl.when(jnp.logical_not(has_up))
    def _():
        ext[0:2, :, 0:cols] = jnp.zeros((2, n + SUB, cols), jnp.float32)

    @pl.when(jnp.logical_not(has_down))
    def _():
        ext[rows + 2 : rows + 4, :, 0:cols] = jnp.zeros((2, n + SUB, cols), jnp.float32)

    def receive_edges(dr, ok_r):
        for dc, ok_c in sides:
            at = (1 + dr) * 2 + (1 if dc > 0 else 0)
            ok = cond(ok_r, ok_c)

            @pl.when(jnp.logical_not(ok))
            def _(at=at):
                nb[at] = jnp.zeros((2 * SUB, LANES), jnp.float32)

            @pl.when(ok)
            def _(dr=dr, dc=dc):
                edge_copy(-dr, -dc).wait_recv()

        at = (1 + dr) * 2
        merged = [
            jnp.where(
                lane % 4 < 2,
                nb[at, h * SUB : (h + 1) * SUB, :],
                nb[at + 1, h * SUB : (h + 1) * SUB, :],
            )
            for h in range(2)
        ]
        pairs = {
            0: [(r + 2, r) for r in range(rows)],
            -1: [(0, rows - 2), (1, rows - 1)],
            1: [(rows + 2, 0), (rows + 3, 1)],
        }[dr]
        for e, r in pairs:
            for g in range(all_groups):
                which, slot = (0, r * groups + g) if g < groups else (1, r)
                ext[e, g * SUB : (g + 1) * SUB, cols:wide] = pltpu.roll(
                    merged[which], (-(4 * slot + 2)) % LANES, 1
                )

    def rotate(src, left, right, first, last):
        def body(e, carry):
            for g in range(groups):
                at = pl.ds(g * SUB, SUB)
                v = src[e, at, :]
                left[e, at, :] = pltpu.roll(v, 1, 1)[:, : left.shape[2]]
                right[e, at, :] = pltpu.roll(v, wide - 1, 1)[:, : right.shape[2]]
            return carry

        lax.fori_loop(first, last, body, 0)

    def apply(srcs, dst, e_first, e_last, w_shift, dst_shift, lane_tiles):
        def body(t, carry):
            across = pl.ds(pl.multiple_of(t * LANES, LANES), LANES)
            window = {}

            def load(e):
                for g in range(groups):
                    for b, src in zip((-1, 0, 1), srcs):
                        window[e, g, b] = src[e, pl.ds(g * SUB, SUB), across]

            load(e_first - 1)
            load(e_first)
            for e in range(e_first, e_last):
                load(e + 1)
                taps = [
                    jnp.broadcast_to(ext[e + w_shift, pl.ds(n + k, 1), across], (SUB, LANES))
                    for k in range(SUB)
                ]
                degree = functools.reduce(jnp.add, taps)
                for g in range(groups):
                    total = degree * window[e, g, 0]
                    for k, (da, db) in enumerate(NEIGHBOURS):
                        total = total + taps[k] * window[e + da, g, db]
                    dst[e + dst_shift, pl.ds(g * SUB, SUB), across] = total
            return carry

        lax.fori_loop(0, lane_tiles, body, 0)

    wide_srcs = (ext_l, ext, ext_r)
    receive_edges(0, None)
    rotate(ext, ext_l, ext_r, 2, rows + 2)
    apply(wide_srcs, y1, 3, rows + 1, 0, -1, tiles + 1)
    receive_edges(-1, has_up)
    receive_edges(1, has_down)

    @pl.when(has_up)
    def _():
        row_copy(True).wait_recv()

    @pl.when(has_down)
    def _():
        row_copy(False).wait_recv()

    rotate(ext, ext_l, ext_r, 0, 2)
    rotate(ext, ext_l, ext_r, rows + 2, rows + 4)
    apply(wide_srcs, y1, 1, 3, 0, -1, tiles + 1)
    apply(wide_srcs, y1, rows + 1, rows + 3, 0, -1, tiles + 1)

    scale = 1.0 / (rows * cols * R * C)

    def gram(load):
        total = jnp.zeros((2 * n, 2 * n), jnp.float32)
        for r in range(rows):
            both = jnp.concatenate(split(load(r)), axis=0)
            total = total + lax.dot_general(both, both, NT, preferred_element_type=jnp.float32)
        half = total[0:n] + total[n : 2 * n]
        square = (half[:, 0:n] + half[:, n : 2 * n]) * scale
        return jnp.concatenate([square[g * SUB : (g + 1) * SUB] for g in range(groups)], axis=1)

    def gather_copies(which, stage, receiving):
        axes, count = stages[stage]
        me = {"row": i, "col": j, "both": i * C + j}[axes]
        copies = []
        for d in range(1, count):
            peer = lax.rem(me + d, count)
            slot = peer if receiving else me
            target = {
                "row": {"row": peer, "col": j},
                "col": {"row": i, "col": peer},
                "both": {"row": lax.div(peer, C), "col": lax.rem(peer, C)},
            }[axes]
            copies.append(pltpu.make_async_remote_copy(
                src_ref=sent.at[which, stage], dst_ref=held.at[which, stage, slot],
                send_sem=gather_send.at[which, stage, d - 1],
                recv_sem=gather_recv.at[which, stage, slot],
                device_id=target, device_id_type=MESH,
            ))
        return copies

    def spread(which, stage, value):
        axes, count = stages[stage]
        me = {"row": i, "col": j, "both": i * C + j}[axes]
        sent[which, stage] = value
        held[which, stage, me] = value
        for copy in gather_copies(which, stage, False):
            copy.start()

    def collect(which, stage):
        for copy in gather_copies(which, stage, True):
            copy.wait_recv()
        terms = [held[which, stage, at] for at in range(stages[stage][1])]
        while len(terms) > 1:
            terms = [sum(terms[k + 1 : k + 2], terms[k]) for k in range(0, len(terms), 2)]
        return terms[0]

    sub = lax.broadcasted_iota(jnp.int32, (SUB, LANES), 0)

    def eliminate(tile, step=4):
        blocks = []
        for g in range(groups):
            mine = tile if g == 0 else pltpu.roll(tile, LANES - g * n, 1)
            eye = (lane - n == sub + g * SUB).astype(jnp.float32)
            blocks.append(jnp.where(lane < n, mine, eye))
        for p in range(0, n, step):
            home, base = p // SUB, p % SUB
            line = [
                jnp.broadcast_to(blocks[home][base + q : base + q + 1, :], (SUB, LANES))
                for q in range(step)
            ]
            column = {
                (s, g): jnp.broadcast_to(blocks[g][:, p + s : p + s + 1], (SUB, LANES))
                for g in range(home, groups)
                for s in range(step)
            }
            corner = {
                (q, s): jnp.broadcast_to(column[s, home][base + q : base + q + 1, :], (SUB, LANES))
                for q in range(step)
                for s in range(q, step)
            }
            scaled = []
            for q in range(step):
                over = 1.0 / corner[q, q]
                scaled.append(line[q] * over)
                ratio = {s: corner[q, s] * over for s in range(q + 1, step)}
                for s in range(q + 1, step):
                    line[s] = line[s] - ratio[s] * line[q]
                    for t in range(s, step):
                        corner[s, t] = corner[s, t] - ratio[s] * corner[q, t]
                    for g in range(home, groups):
                        column[s, g] = column[s, g] - ratio[s] * column[q, g]
            for g in range(home, groups):
                if g == home and base + step == SUB:
                    continue
                update = column[0, g] * scaled[0]
                for q in range(1, step):
                    update = update + column[q, g] * scaled[q]
                if g == home:
                    update = jnp.where(sub >= base + step, update, 0.0)
                blocks[g] = blocks[g] - update
            for q in range(step):
                done = line[q] * (1.0 / jnp.sqrt(corner[q, q]))
                blocks[home] = jnp.where(sub == base + q, done, blocks[home])
        return jnp.concatenate(blocks, axis=0)

    spread(0, 0, gram(lambda r: y1[r + 1, :, 0:cols]))
    rotate(y1, y1_l, y1_r, 0, rows + 2)
    apply((y1_l, y1, y1_r), y2, 1, rows + 1, 1, -1, tiles)
    spread(1, 0, gram(lambda r: y2[r]))
    for stage in range(1, len(stages)):
        spread(0, stage, collect(0, stage - 1))
        spread(1, stage, collect(1, stage - 1))
    table_1 = eliminate(collect(0, len(stages) - 1))
    table_2 = eliminate(collect(1, len(stages) - 1))

    tables[0] = table_1
    tables[1] = table_2

    for dr, ok_r in ups:
        for dc, ok_c in sides:
            @pl.when(cond(ok_r, ok_c))
            def _(dr=dr, dc=dc):
                edge_copy(dr, dc).wait_send()

    @pl.when(has_down)
    def _():
        row_copy(True).wait_send()

    @pl.when(has_up)
    def _():
        row_copy(False).wait_send()

    for which in range(2):
        for stage in range(len(stages)):
            for copy in gather_copies(which, stage, False):
                copy.wait_send()


def finish(n, rows, cols, y2, tables, out_ref, fac_ref, staged, store_sem):
    groups = n // SUB
    tiles = cols // LANES
    inverse_1 = tables[0, :, n : 2 * n]
    upper_2 = tables[1, :, 0:n]
    inverse_2 = tables[1, :, n : 2 * n]
    row_at = lax.broadcasted_iota(jnp.int32, (n, n), 0)
    col_at = lax.broadcasted_iota(jnp.int32, (n, n), 1)
    upper_2 = jnp.where(col_at >= row_at, upper_2, 0.0)
    last = lax.dot_general(
        upper_2, inverse_1, NT, precision=HIGHEST, preferred_element_type=jnp.float32
    )
    fac_ref[...] = jnp.where(col_at >= row_at, last, 0.0)

    inv_hi, inv_lo = split(inverse_2)
    left = jnp.concatenate([inv_hi, inv_lo, inv_hi], axis=1)
    stores = []
    for t0 in range(0, tiles, 2):
        for r in range(rows):
            hi, lo = split(y2[r, :, t0 * LANES : (t0 + 2) * LANES])
            right = jnp.concatenate([hi, hi, lo], axis=0)
            solved = jnp.dot(left, right, preferred_element_type=jnp.float32)
            for t in range(2):
                for g in range(groups):
                    staged[t0 + t, pl.ds(g * SUB * rows + r, SUB, stride=rows), :] = solved[
                        g * SUB : (g + 1) * SUB, t * LANES : (t + 1) * LANES
                    ]
        for t in range(t0, t0 + 2):
            stores.append(pltpu.make_async_copy(
                staged.at[t], out_ref.at[:, pl.ds(t * LANES, LANES)], store_sem.at[t]
            ))
            stores[-1].start()
    for store in stores:
        store.wait()


def on_device(sketch, weights):
    n, rows, cols = sketch.shape
    R, C = lax.axis_size("row"), lax.axis_size("col")
    stages = (("both", R * C),) if R * C <= 16 else (("row", R), ("col", C))
    peers = max(count for _, count in stages)
    dma = pltpu.SemaphoreType.DMA
    f32 = jnp.float32
    image, tables = pl.pallas_call(
        functools.partial(kernel, n, rows, cols, R, C, stages),
        out_shape=(
            jax.ShapeDtypeStruct((rows, n, cols), f32),
            jax.ShapeDtypeStruct((2, n, LANES), f32),
        ),
        in_specs=[pl.BlockSpec(memory_space=pltpu.HBM)] * 2,
        out_specs=(
            pl.BlockSpec(memory_space=pltpu.VMEM),
            pl.BlockSpec(memory_space=pltpu.VMEM),
        ),
        scratch_shapes=[
            pltpu.VMEM((cols // LANES, n * rows, LANES), f32),
            pltpu.VMEM((cols // LANES, SUB * rows, LANES), f32),
            pltpu.VMEM((rows + 4, n + SUB, cols + LANES), f32),
            pltpu.VMEM((rows + 4, n, cols + LANES), f32),
            pltpu.VMEM((rows + 4, n, cols + LANES), f32),
            pltpu.VMEM((rows + 2, n, cols + LANES), f32),
            pltpu.VMEM((rows + 2, n, cols), f32),
            pltpu.VMEM((rows + 2, n, cols), f32),
            pltpu.VMEM((2 * SUB, LANES), f32),
            pltpu.VMEM((6, 2 * SUB, LANES), f32),
            pltpu.VMEM((2, len(stages), peers, SUB, LANES), f32),
            pltpu.VMEM((2, len(stages), SUB, LANES), f32),
            dma((2, cols // LANES)), dma((2,)), dma((2,)), dma((6,)), dma((6,)),
            dma((2, len(stages), peers)), dma((2, len(stages), peers)),
        ],
        compiler_params=pltpu.CompilerParams(
            collective_id=0, has_side_effects=True, vmem_limit_bytes=62 * 1024 * 1024
        ),
    )(sketch.reshape(n * rows, cols), weights.reshape(SUB * rows, cols))
    basis, factor = pl.pallas_call(
        functools.partial(finish, n, rows, cols),
        out_shape=(
            jax.ShapeDtypeStruct((n * rows, cols), f32),
            jax.ShapeDtypeStruct((n, n), f32),
        ),
        in_specs=[pl.BlockSpec(memory_space=pltpu.VMEM)] * 2,
        out_specs=(
            pl.BlockSpec(memory_space=pl.ANY),
            pl.BlockSpec(memory_space=pltpu.VMEM),
        ),
        scratch_shapes=[
            pltpu.VMEM((cols // LANES, n * rows, LANES), f32),
            dma((cols // LANES,)),
        ],
        compiler_params=pltpu.CompilerParams(vmem_limit_bytes=62 * 1024 * 1024),
    )(image, tables)
    return basis.reshape(n, rows, cols), factor


def solution(mesh):
    return jax.shard_map(
        on_device,
        mesh=mesh,
        in_specs=(P(None, ("sec", "row"), "col"), P(None, ("sec", "row"), "col")),
        out_specs=(P(None, ("sec", "row"), "col"), P("sec", None)),
        check_vma=False,
    )
```

profile of v0, /device:TPU:0, one launch (start us, length us, event | category | flops | bytes accessed | tf_op | source)
XLA Modules:
  0.0 23.3 jit_solution(1405212625821541785)
XLA Ops:
  0.6 19.9 %shard_map.41 = (f32[8,32,512]{2,1,0:T(8,128)}, f32[2,32,128]{2,1,0:T(8,128)}) custom-call(f32[256,512]{1,0:T(8,128)} %bitcast.3, f32[64,512]{1,0:T(8,128)} %bitcast.4), custom_call_target="tpu_custom_call" | custom-call | tf_op jit(solution)/shard_map/pallas_call | solution.py:412
  20.5 2.7 %shard_map.42 = (f32[256,512]{1,0:T(8,128)}, f32[32,32]{1,0:T(8,128)}) custom-call(f32[8,32,512]{2,1,0:T(8,128)} %get-tuple-element.6.y2, f32[2,32,128]{2,1,0:T(8,128)} %get-tuple-element.7.tables), custom_call_target="tpu_custom_call" | custom-call | tf_op jit(solution)/shard_map/pallas_call | solution.py:443
where the time goes:
time: 23.4 us; the launch traced here: 23.3 us
  Pallas kernels  22.6 us (97%)
  between operations  0.64 us (3%)
    pallas_call x1, Pallas kernels, on_device(): pl.pallas_call(functools.partial(kernel, n, rows, cols, R, C, stages), ou...  19.9 us
    pallas_call x1, Pallas kernels, on_device(): pl.pallas_call(functools.partial(finish, n, rows, cols), out_shape=(jax.S...  2.74 us

commit v1 on v0

v1 whole, which is shorter than its diff:
```python
import functools

import jax
import jax.numpy as jnp
from jax import lax
from jax.experimental import pallas as pl
from jax.experimental.pallas import tpu as pltpu
from jax.sharding import PartitionSpec as P

LANES = 128
SUB = 8
MESH = pl.DeviceIdType.MESH
NT = (((1,), (1,)), ((), ()))
HIGHEST = lax.Precision.HIGHEST
f32 = jnp.float32
bf16 = jnp.bfloat16


def split(x):
    hi = x.astype(bf16)
    lo = (x - hi.astype(f32)).astype(bf16)
    return hi, lo


def kernel(
    n, rows, cols, R, C, stages, rounds,
    sk_hbm, w_hbm, y2_out, tables,
    raw, wraw, x, w, ws, y1, y2, pack, nb, held, sent,
    load_sem, col_send, col_recv, row_send, row_recv, gather_send, gather_recv, reach,
):
    groups = n // SUB
    tiles = cols // LANES
    i = lax.axis_index("row")
    j = lax.axis_index("col")
    has_up, has_down = i > 0, i < R - 1
    has_left, has_right = j > 0, j < C - 1

    def cond(*terms):
        terms = [t for t in terms if t is not None]
        return functools.reduce(jnp.logical_and, terms)

    ups = {-1: has_up, 0: None, 1: has_down}
    sides = {-1: has_left, 0: None, 1: has_right}
    around = [(dr, dc) for dr in (0, -1, 1) for dc in (-1, 1)] + [(-1, 0), (1, 0)]

    def at_offset(dr, dc):
        return {"row": i + dr, "col": j + dc}

    def greet(sem):
        for dr, dc in around:
            @pl.when(cond(ups[dr], sides[dc]))
            def _(dr=dr, dc=dc):
                pl.semaphore_signal(sem, inc=1, device_id=at_offset(dr, dc), device_id_type=MESH)

    height = 1 + has_up.astype(jnp.int32) + has_down.astype(jnp.int32)
    breadth = 1 + has_left.astype(jnp.int32) + has_right.astype(jnp.int32)
    neighbours = height * breadth - 1

    barrier = pltpu.get_barrier_semaphore()
    greet(barrier)

    loads = []
    for t in range(tiles):
        across = pl.ds(t * LANES, LANES)
        loads.append(pltpu.make_async_copy(sk_hbm.at[:, across], raw.at[t], load_sem.at[0, t]))
        loads.append(pltpu.make_async_copy(w_hbm.at[:, across], wraw.at[t], load_sem.at[1, t]))
    for load in loads:
        load.start()

    lane = lax.broadcasted_iota(jnp.int32, (SUB, LANES), 1)
    sub = lax.broadcasted_iota(jnp.int32, (SUB, LANES), 0)

    with jax.named_scope("load"):
        for load in loads:
            load.wait()
    with jax.named_scope("relayout"):
        for t in range(tiles):
            for r in range(rows):
                for g in range(groups):
                    x[t, r + 2, g * SUB : (g + 1) * SUB, :] = raw[
                        t, pl.ds(g * SUB * rows + r, SUB, stride=rows), :
                    ]
                w[t, r + 1] = wraw[t, pl.ds(r, SUB, stride=rows), :]

    outer = [0, 1, rows - 2, rows - 1]
    inner = list(range(2, rows - 2))
    halves = (outer, inner)

    with jax.named_scope("pack"):
        for h, members in enumerate(halves):
            packed = jnp.zeros((SUB, LANES), f32)
            for at, r in enumerate(members):
                for g in range(groups + 1):
                    if g < groups:
                        slot = at * groups + g
                        first = x[0, r + 2, g * SUB : (g + 1) * SUB, :]
                        final = x[tiles - 1, r + 2, g * SUB : (g + 1) * SUB, :]
                    else:
                        slot = len(members) * groups + at
                        first, final = w[0, r + 1], w[tiles - 1, r + 1]
                    edge = jnp.where(lane < LANES // 2, first, final)
                    moved = pltpu.roll(edge, (4 * slot + 2) % LANES, 1)
                    packed = jnp.where(lane // 4 == slot, moved, packed)
            pack[h * SUB : (h + 1) * SUB, :] = packed

    def edge_copy(dr, dc):
        at = (1 - dr) * 2 + (0 if dc > 0 else 1)
        size = 2 * SUB if dr == 0 else SUB
        return pltpu.make_async_remote_copy(
            src_ref=pack.at[pl.ds(0, size)], dst_ref=nb.at[at, pl.ds(0, size)],
            send_sem=col_send.at[at], recv_sem=col_recv.at[at],
            device_id=at_offset(dr, dc), device_id_type=MESH,
        )

    def row_copies(dr):
        src = 2 if dr < 0 else rows
        dst = rows + 2 if dr < 0 else 0
        at = 1 if dr < 0 else 0
        refs = [(
            w.at[pl.ds(0, tiles), 1 if dr < 0 else rows],
            w.at[pl.ds(0, tiles), rows + 1 if dr < 0 else 0],
        )]
        for t in range(tiles):
            refs.append((x.at[t, pl.ds(src, 2)], x.at[t, pl.ds(dst, 2)]))
        return [
            pltpu.make_async_remote_copy(
                src_ref=a, dst_ref=b, send_sem=row_send.at[at, k], recv_sem=row_recv.at[at, k],
                device_id=at_offset(dr, 0), device_id_type=MESH,
            )
            for k, (a, b) in enumerate(refs)
        ]

    with jax.named_scope("barrier"):
        pl.semaphore_wait(barrier, neighbours)
    with jax.named_scope("sends"):
        for dr, dc in around[:6]:
            @pl.when(cond(ups[dr], sides[dc]))
            def _(dr=dr, dc=dc):
                edge_copy(dr, dc).start()
        for dr in (-1, 1):
            @pl.when(ups[dr])
            def _(dr=dr):
                for copy in row_copies(dr):
                    copy.start()
        if rounds > 1:
            greet(reach.at[0])

    for dr in (-1, 1):
        @pl.when(jnp.logical_not(ups[dr]))
        def _(dr=dr):
            e = 0 if dr < 0 else rows + 2
            for t in range(tiles):
                x[t, e : e + 2] = jnp.zeros((2, n, LANES), f32)
                w[t, 0 if dr < 0 else rows + 1] = jnp.zeros((SUB, LANES), f32)
    for dr, dc in around[:6]:
        at = (1 + dr) * 2 + (1 if dc > 0 else 0)
        @pl.when(jnp.logical_not(cond(ups[dr], sides[dc])))
        def _(at=at):
            nb[at] = jnp.zeros((2 * SUB, LANES), f32)

    edge = tiles
    main = list(range(tiles))
    taken = (lane >= LANES - 2) | ((lane >= 64) & (lane < 66))

    def merge(at, h):
        part = pl.ds(h * SUB, SUB)
        return jnp.where(lane % 4 < 2, nb[at, part, :], pltpu.roll(nb[at + 1, part, :], 64, 1))

    def unpack(both, slot):
        return pltpu.roll(both, (-(4 * slot + 2)) % LANES, 1)

    def near(first, final):
        return jnp.where((lane >= 32) & (lane < 96), pltpu.roll(final, 64, 1), first)

    def shift_weights(r, ring):
        size = len(ring)
        taps = [w[t, r + 1] for t in ring]
        ahead = [pltpu.roll(v, LANES - 1, 1) for v in taps]
        behind = [pltpu.roll(v, 1, 1) for v in taps]
        left_taps = (sub == 0) | (sub == 3) | (sub == 5)
        right_taps = (sub == 2) | (sub == 4) | (sub == 7)
        for k, t in enumerate(ring):
            after, before = ahead[k], behind[k]
            if size > 1:
                after = jnp.where(lane == LANES - 1, ahead[(k + 1) % size], after)
                before = jnp.where(lane == 0, behind[k - 1], before)
            ws[t, r + 1, 0:SUB, :] = jnp.where(
                left_taps, after, jnp.where(right_taps, before, taps[k])
            )
            degree = jnp.sum(taps[k], axis=0, keepdims=True)
            ws[t, r + 1, SUB : 2 * SUB, :] = jnp.broadcast_to(degree, (SUB, LANES))

    def stencil(src, e, dst, d, r, ring):
        size = len(ring)
        parts = {}

        def write(k, g):
            center, low, high = parts[k, g]
            if size > 1:
                low = jnp.where(lane == 0, parts[(k - 1) % size, g][1], low)
                high = jnp.where(lane == LANES - 1, parts[(k + 1) % size, g][2], high)
            dst[ring[k], d, g * SUB : (g + 1) * SUB, :] = center + low + high

        for k, t in enumerate(ring):
            tap = [
                jnp.broadcast_to(ws[t, r + 1, pl.ds(q, 1), :], (SUB, LANES)) for q in range(SUB)
            ]
            degree = ws[t, r + 1, SUB : 2 * SUB, :]
            for g in range(groups):
                part = slice(g * SUB, (g + 1) * SUB)
                up, here, down = src[t, e - 1, part, :], src[t, e, part, :], src[t, e + 1, part, :]
                parts[k, g] = (
                    degree * here + tap[1] * up + tap[6] * down,
                    pltpu.roll(tap[0] * up + tap[3] * here + tap[5] * down, 1, 1),
                    pltpu.roll(tap[2] * up + tap[4] * here + tap[7] * down, LANES - 1, 1),
                )
                if k >= 2:
                    write(k - 1, g)
        for k in sorted({0, size - 1}):
            for g in range(groups):
                write(k, g)

    def gram(src, picks):
        pieces = []
        for d, with_main, with_edge in picks:
            if with_main:
                for t in main:
                    v = src[t, d]
                    if t == 0:
                        v = jnp.where(wide_lane >= 2, v, 0.0)
                    if t == tiles - 1:
                        v = jnp.where(wide_lane < LANES - 2, v, 0.0)
                    pieces.append(v)
            if with_edge:
                pieces.append(jnp.where(wide_edge, src[edge, d], 0.0))
        both = jnp.concatenate(split(jnp.concatenate(pieces, axis=1)), axis=0)
        return lax.dot_general(both, both, NT, preferred_element_type=f32)

    wide_lane = lax.broadcasted_iota(jnp.int32, (n, LANES), 1)
    wide_edge = (wide_lane < 2) | ((wide_lane >= 62) & (wide_lane < 64))

    with jax.named_scope("weights"):
        for r in range(rows):
            shift_weights(r, main)
    with jax.named_scope("y1in"):
        for r in range(1, rows - 1):
            stencil(x, r + 2, y1, r + 1, r, main)
    with jax.named_scope("y2in"):
        for r in range(2, rows - 2):
            stencil(y1, r + 1, y2, r, r, main)
    with jax.named_scope("nearedge"):
        for r in range(rows):
            for g in range(groups):
                part = slice(g * SUB, (g + 1) * SUB)
                x[edge, r + 2, part, :] = near(x[0, r + 2, part, :], x[tiles - 1, r + 2, part, :])
            w[edge, r + 1] = near(w[0, r + 1], w[tiles - 1, r + 1])
    with jax.named_scope("gramin"):
        total_1 = gram(y1, [(r + 1, True, False) for r in range(1, rows - 1)])
        total_2 = gram(y2, [(r, True, False) for r in range(2, rows - 2)])

    if rounds > 1:
        with jax.named_scope("round2"):
            pl.semaphore_wait(reach.at[0], neighbours)
            if rounds > 2:
                greet(reach.at[1])

    with jax.named_scope("recvcols"):
        for dc in (-1, 1):
            @pl.when(sides[dc])
            def _(dc=dc):
                edge_copy(0, -dc).wait_recv()
    with jax.named_scope("edges"):
        for h, members in enumerate(halves):
            both = merge(2, h)
            for at, r in enumerate(members):
                for g in range(groups):
                    part = slice(g * SUB, (g + 1) * SUB)
                    x[edge, r + 2, part, :] = jnp.where(
                        taken, unpack(both, at * groups + g), x[edge, r + 2, part, :]
                    )
                w[edge, r + 1] = jnp.where(
                    taken, unpack(both, len(members) * groups + at), w[edge, r + 1]
                )
        for r in range(rows):
            shift_weights(r, [edge])
        for r in range(1, rows - 1):
            stencil(x, r + 2, y1, r + 1, r, [edge])
        for r in range(2, rows - 2):
            stencil(y1, r + 1, y2, r, r, [edge])
        total_1 = total_1 + gram(y1, [(r + 1, False, True) for r in range(1, rows - 1)])
        total_2 = total_2 + gram(y2, [(r, False, True) for r in range(2, rows - 2)])

    def side(step, carry):
        total_1, total_2 = carry
        low = lax.rem(i + 1 + step, 2)
        for dr in (-1, 1):
            @pl.when(cond(low == (0 if dr < 0 else 1), ups[dr]))
            def _(dr=dr):
                for dc in (-1, 1):
                    @pl.when(sides[dc])
                    def _(dc=dc):
                        edge_copy(-dr, -dc).wait_recv()
                for copy in row_copies(-dr):
                    copy.wait_recv()
        both = merge(low * 4, 0)
        tap_both = jnp.where(
            low == 0, unpack(both, 4 * groups + 3), unpack(both, 4 * groups)
        )
        both = jnp.where(low == 0, pltpu.roll(both, LANES - 8 * groups, 1), both)
        for k in range(2):
            e = low * (rows + 2) + k
            for g in range(groups):
                part = slice(g * SUB, (g + 1) * SUB)
                x[edge, e, part, :] = jnp.where(
                    taken, unpack(both, k * groups + g),
                    near(x[0, e, part, :], x[tiles - 1, e, part, :]),
                )
        e = low * (rows + 1)
        w[edge, e] = jnp.where(taken, tap_both, near(w[0, e], w[tiles - 1, e]))
        for ring in (main, [edge]):
            shift_weights(e - 1, ring)
        for ring in (main, [edge]):
            for k in range(2):
                r = low * rows - 1 + k
                stencil(x, r + 2, y1, r + 1, r, ring)
        for ring in (main, [edge]):
            for k in range(2):
                r = low * (rows - 2) + k
                stencil(y1, r + 1, y2, r, r, ring)
        total_1 = total_1 + gram(y1, [(low * (rows - 1) + 1, True, True)])
        total_2 = total_2 + gram(y2, [(low * (rows - 2) + k, True, True) for k in range(2)])
        return total_1, total_2

    with jax.named_scope("sides"):
        total_1, total_2 = lax.fori_loop(0, 2, side, (total_1, total_2))

    scale = 1.0 / (rows * cols * R * C)

    def fold(total):
        half = total[0:n] + total[n : 2 * n]
        square = (half[:, 0:n] + half[:, n : 2 * n]) * scale
        return jnp.concatenate([square[g * SUB : (g + 1) * SUB] for g in range(groups)], axis=1)

    def gather_copies(stage, receiving):
        axes, count = stages[stage]
        me = {"row": i, "col": j, "both": j * R + i}[axes]
        copies = []
        for k in range(count - 1):
            peer = k + (k >= me).astype(jnp.int32)
            slot = peer if receiving else me
            target = {
                "row": {"row": peer, "col": j},
                "col": {"row": i, "col": peer},
                "both": {"row": lax.rem(peer, R), "col": lax.div(peer, R)},
            }[axes]
            copies.append(pltpu.make_async_remote_copy(
                src_ref=sent.at[stage], dst_ref=held.at[stage, slot],
                send_sem=gather_send.at[stage, k],
                recv_sem=gather_recv.at[stage, slot],
                device_id=target, device_id_type=MESH,
            ))
        return copies

    def spread(stage, value):
        axes, count = stages[stage]
        me = {"row": i, "col": j, "both": j * R + i}[axes]
        sent[stage] = value
        held[stage, me] = value
        for copy in gather_copies(stage, False):
            copy.start()

    def collect(stage):
        for copy in gather_copies(stage, True):
            copy.wait_recv()
        terms = [held[stage, at] for at in range(stages[stage][1])]
        while len(terms) > 1:
            terms = [sum(terms[k + 1 : k + 2], terms[k]) for k in range(0, len(terms), 2)]
        return terms[0]

    with jax.named_scope("fold"):
        value = jnp.concatenate([fold(total_1), fold(total_2)], axis=0)
    for k in range(2, rounds):
        with jax.named_scope("round3"):
            pl.semaphore_wait(reach.at[k - 1], neighbours)
            if k + 1 < rounds:
                greet(reach.at[k])
    with jax.named_scope("spread"):
        spread(0, value)

    def eliminate(square, step=4):
        blocks = []
        half = lane % 64
        for g in range(groups):
            mine_1, mine_2 = square[0:SUB], square[SUB : 2 * SUB]
            if g > 0:
                mine_1 = pltpu.roll(mine_1, LANES - g * n, 1)
            if g != 2:
                mine_2 = pltpu.roll(mine_2, (64 - g * n) % LANES, 1)
            eye = (half - n == sub + g * SUB).astype(f32)
            blocks.append(jnp.where(half < n, jnp.where(lane < 64, mine_1, mine_2), eye))

        def over_lanes(v, p):
            return jnp.where(
                lane < 64,
                jnp.broadcast_to(v[:, p : p + 1], (SUB, LANES)),
                jnp.broadcast_to(v[:, 64 + p : 64 + p + 1], (SUB, LANES)),
            )

        for p in range(0, n, step):
            home, base = p // SUB, p % SUB
            line = [
                jnp.broadcast_to(blocks[home][base + q : base + q + 1, :], (SUB, LANES))
                for q in range(step)
            ]
            column = {
                (s, g): over_lanes(blocks[g], p + s)
                for g in range(home, groups)
                for s in range(step)
            }
            corner = {
                (q, s): jnp.broadcast_to(column[s, home][base + q : base + q + 1, :], (SUB, LANES))
                for q in range(step)
                for s in range(q, step)
            }
            scaled = []
            for q in range(step):
                over = 1.0 / corner[q, q]
                scaled.append(line[q] * over)
                ratio = {s: corner[q, s] * over for s in range(q + 1, step)}
                for s in range(q + 1, step):
                    line[s] = line[s] - ratio[s] * line[q]
                    for t in range(s, step):
                        corner[s, t] = corner[s, t] - ratio[s] * corner[q, t]
                    for g in range(home, groups):
                        column[s, g] = column[s, g] - ratio[s] * column[q, g]
            for g in range(home, groups):
                if g == home and base + step == SUB:
                    continue
                update = column[0, g] * scaled[0]
                for q in range(1, step):
                    update = update + column[q, g] * scaled[q]
                if g == home:
                    update = jnp.where(sub >= base + step, update, 0.0)
                blocks[g] = blocks[g] - update
            for q in range(step):
                done = line[q] * (1.0 / jnp.sqrt(corner[q, q]))
                blocks[home] = jnp.where(sub == base + q, done, blocks[home])
        return jnp.concatenate(blocks, axis=0)

    for stage in range(1, len(stages)):
        spread(stage, collect(stage - 1))
    with jax.named_scope("patch"):
        for r in range(rows):
            edges = y2[edge, r]
            pieces = [y2[t, r] for t in main]
            pieces[0] = jnp.where(wide_lane < 2, edges, pieces[0])
            pieces[-1] = jnp.where(wide_lane >= LANES - 2, pltpu.roll(edges, 64, 1), pieces[-1])
            y2_out[r] = jnp.concatenate(split(jnp.concatenate(pieces, axis=1)), axis=0)
    with jax.named_scope("collect"):
        square = collect(len(stages) - 1)
    with jax.named_scope("eliminate"):
        tables[...] = eliminate(square)

    with jax.named_scope("drain"):
        for dr, dc in around[:6]:
            @pl.when(cond(ups[dr], sides[dc]))
            def _(dr=dr, dc=dc):
                edge_copy(dr, dc).wait_send()
        for dr in (-1, 1):
            @pl.when(ups[dr])
            def _(dr=dr):
                for copy in row_copies(dr):
                    copy.wait_send()
        for stage in range(len(stages)):
            for copy in gather_copies(stage, False):
                copy.wait_send()


def finish(n, rows, cols, y2, tables, out_ref, fac_ref, staged, fac, store_sem):
    groups = n // SUB
    tiles = cols // LANES
    inv_hi, inv_lo = split(tables[:, 3 * n : 4 * n])
    left = jnp.concatenate([inv_hi, inv_lo, inv_hi], axis=1)
    stores = []
    for t0 in range(0, tiles, 2):
        for r in range(rows):
            hi = y2[r, 0:n, t0 * LANES : (t0 + 2) * LANES]
            lo = y2[r, n : 2 * n, t0 * LANES : (t0 + 2) * LANES]
            right = jnp.concatenate([hi, hi, lo], axis=0)
            solved = jnp.dot(left, right, preferred_element_type=f32)
            for t in range(2):
                for g in range(groups):
                    staged[t0 + t, pl.ds(g * SUB * rows + r, SUB, stride=rows), :] = solved[
                        g * SUB : (g + 1) * SUB, t * LANES : (t + 1) * LANES
                    ]
        for t in range(t0, t0 + 2):
            stores.append(pltpu.make_async_copy(
                staged.at[t], out_ref.at[:, pl.ds(t * LANES, LANES)], store_sem.at[t]
            ))
            stores[-1].start()
    inverse_1 = tables[:, n : 2 * n]
    upper_2 = tables[:, 2 * n : 3 * n]
    row_at = lax.broadcasted_iota(jnp.int32, (n, n), 0)
    col_at = lax.broadcasted_iota(jnp.int32, (n, n), 1)
    upper_2 = jnp.where(col_at >= row_at, upper_2, 0.0)
    last = lax.dot_general(upper_2, inverse_1, NT, precision=HIGHEST, preferred_element_type=f32)
    fac[...] = jnp.where(col_at >= row_at, last, 0.0)
    stores.append(pltpu.make_async_copy(fac, fac_ref, store_sem.at[tiles]))
    stores[-1].start()
    for store in stores:
        store.wait()


def on_device(sketch, weights):
    n, rows, cols = sketch.shape
    R, C = lax.axis_size("row"), lax.axis_size("col")
    tiles = cols // LANES
    stages = (("both", R * C),) if R * C <= 16 else (("row", R), ("col", C))
    rounds = max(R, C) - 1
    peers = max(count for _, count in stages)
    dma = pltpu.SemaphoreType.DMA
    image, tables = pl.pallas_call(
        functools.partial(kernel, n, rows, cols, R, C, stages, rounds),
        out_shape=(
            pltpu.VMEM((rows, 2 * n, cols), bf16),
            pltpu.VMEM((n, LANES), f32),
        ),
        in_specs=[pl.BlockSpec(memory_space=pltpu.HBM)] * 2,
        out_specs=(
            pl.BlockSpec(memory_space=pltpu.VMEM),
            pl.BlockSpec(memory_space=pltpu.VMEM),
        ),
        scratch_shapes=[
            pltpu.VMEM((tiles, n * rows, LANES), f32),
            pltpu.VMEM((tiles, SUB * rows, LANES), f32),
            pltpu.VMEM((tiles + 1, rows + 4, n, LANES), f32),
            pltpu.VMEM((tiles + 1, rows + 2, SUB, LANES), f32),
            pltpu.VMEM((tiles + 1, rows + 2, 2 * SUB, LANES), f32),
            pltpu.VMEM((tiles + 1, rows + 2, n, LANES), f32),
            pltpu.VMEM((tiles + 1, rows, n, LANES), f32),
            pltpu.VMEM((2 * SUB, LANES), f32),
            pltpu.VMEM((6, 2 * SUB, LANES), f32),
            pltpu.VMEM((len(stages), peers, 2 * SUB, LANES), f32),
            pltpu.VMEM((len(stages), 2 * SUB, LANES), f32),
            dma((2, tiles)), dma((6,)), dma((6,)), dma((2, tiles + 1)), dma((2, tiles + 1)),
            dma((len(stages), peers)), dma((len(stages), peers)),
            pltpu.SemaphoreType.REGULAR((max(rounds - 1, 1),)),
        ],
        compiler_params=pltpu.CompilerParams(
            collective_id=0, has_side_effects=True, vmem_limit_bytes=16 * 1024 * 1024
        ),
    )(
        pltpu.with_memory_space_constraint(sketch.reshape(n * rows, cols), pltpu.HBM),
        pltpu.with_memory_space_constraint(weights.reshape(SUB * rows, cols), pltpu.HBM),
    )
    basis, factor = pl.pallas_call(
        functools.partial(finish, n, rows, cols),
        out_shape=(
            jax.ShapeDtypeStruct((n * rows, cols), f32),
            jax.ShapeDtypeStruct((n, n), f32),
        ),
        in_specs=[pl.BlockSpec(memory_space=pltpu.VMEM)] * 2,
        out_specs=(
            pl.BlockSpec(memory_space=pl.ANY),
            pl.BlockSpec(memory_space=pl.ANY),
        ),
        scratch_shapes=[
            pltpu.VMEM((tiles, n * rows, LANES), f32),
            pltpu.VMEM((n, n), f32),
            dma((tiles + 1,)),
        ],
        compiler_params=pltpu.CompilerParams(vmem_limit_bytes=16 * 1024 * 1024),
    )(image, tables)
    return basis.reshape(n, rows, cols), factor


def solution(mesh):
    return jax.shard_map(
        on_device,
        mesh=mesh,
        in_specs=(P(None, ("sec", "row"), "col"), P(None, ("sec", "row"), "col")),
        out_specs=(P(None, ("sec", "row"), "col"), P("sec", None)),
        check_vma=False,
    )
```

time: 23.4 us -> 18 us (0.77)
  Pallas kernels: 22.6 us -> 17.2 us
    pallas_call x1, Pallas kernels: 19.9 us -> 16.1 us  [on_device(): pl.pallas_call(functools.partial(kernel, n, rows, cols, R, C, stages, rou...]
    pallas_call x1, Pallas kernels: 2.74 us -> 1.11 us  [on_device(): pl.pallas_call(functools.partial(finish, n, rows, cols), out_shape=(jax.S...]
where the time goes in v1:
time: 18 us; the launch traced here: 17.8 us
  Pallas kernels  17.2 us (96%)
  between operations  0.64 us (4%)
    pallas_call x1, Pallas kernels, on_device(): pl.pallas_call(functools.partial(kernel, n, rows, cols, R, C, stages, rou...  16.1 us
    pallas_call x1, Pallas kernels, on_device(): pl.pallas_call(functools.partial(finish, n, rows, cols), out_shape=(jax.S...  1.11 us

profile of v1, /device:TPU:0, one launch (start us, length us, event | category | flops | bytes accessed | tf_op | source)
XLA Modules:
  0.0 17.8 jit_solution(1723102508916438485)
XLA Ops:
  0.6 16.1 %shard_map.41 = (bf16[8,64,512]{2,1,0:T(8,128)(2,1)S(1)}, f32[32,128]{1,0:T(8,128)S(1)}) custom-call(f32[256,512]{1,0:T(8,128)} %bitcast.3, f32[64,512]{1,0:T(8,128)} %bitcast.4), custom_call_target="tpu_custom_call" | custom-call | tf_op jit(solution)/shard_map/pallas_call | solution.py:522
  16.7 1.1 %shard_map.42 = (f32[256,512]{1,0:T(8,128)}, f32[32,32]{1,0:T(8,128)}) custom-call(bf16[8,64,512]{2,1,0:T(8,128)(2,1)S(1)} %get-tuple-element.6.y2, f32[32,128]{1,0:T(8,128)S(1)} %get-tuple-element.7.tables), custom_call_target="tpu_custom_call" | custom-call | tf_op jit(solution)/shard_map/pallas_call | solution.py:556

commit v2 on v1

v2 whole, which is shorter than its diff:
```python
import functools

import jax
import jax.numpy as jnp
from jax import lax
from jax.experimental import pallas as pl
from jax.experimental.pallas import tpu as pltpu
from jax.sharding import PartitionSpec as P

LANES = 128
SUB = 8
MESH = pl.DeviceIdType.MESH
NT = (((1,), (1,)), ((), ()))
HIGHEST = lax.Precision.HIGHEST
f32 = jnp.float32
bf16 = jnp.bfloat16


def split(x):
    hi = x.astype(bf16)
    lo = (x - hi.astype(f32)).astype(bf16)
    return hi, lo


def kernel(
    n, rows, cols, R, C, stages, rounds,
    sk_hbm, w_hbm, y2_out, tables,
    raw, wraw, x, w, ws, y1, y2, pack, nb, held, sent,
    load_sem, col_send, col_recv, row_send, row_recv, gather_send, gather_recv, reach,
):
    groups = n // SUB
    tiles = cols // LANES
    i = lax.axis_index("row")
    j = lax.axis_index("col")
    flip = 1 - lax.rem(i, 2)
    near_i = i + 2 * flip - 1
    far_i = i + 1 - 2 * flip
    has_far = (far_i >= 0) & (far_i < R)
    has_left, has_right = j > 0, j < C - 1

    kinds = ((i, None), (near_i, None), (far_i, has_far))
    SAME, NEAR, FAR = range(3)
    sides = {-1: has_left, 0: None, 1: has_right}
    beside = [(FAR, 0), (NEAR, 0)]
    around = [(kind, dc) for kind in (SAME, FAR, NEAR) for dc in (-1, 1)]

    def when(kind, dc):
        terms = [t for t in (kinds[kind][1], sides[dc]) if t is not None]
        if not terms:
            return lambda body: body()
        return pl.when(functools.reduce(jnp.logical_and, terms))

    def unless(kind, dc):
        terms = [t for t in (kinds[kind][1], sides[dc]) if t is not None]
        if not terms:
            return lambda body: None
        return pl.when(jnp.logical_not(functools.reduce(jnp.logical_and, terms)))

    def at_offset(kind, dc):
        return {"row": kinds[kind][0], "col": j + dc}

    def greet(sem):
        for kind, dc in beside + around:
            @when(kind, dc)
            def _(kind=kind, dc=dc):
                pl.semaphore_signal(sem, inc=1, device_id=at_offset(kind, dc), device_id_type=MESH)

    height = 2 + has_far.astype(jnp.int32)
    breadth = 1 + has_left.astype(jnp.int32) + has_right.astype(jnp.int32)
    neighbours = height * breadth - 1

    barrier = pltpu.get_barrier_semaphore()
    greet(barrier)

    loads = []
    for t in range(tiles):
        across = pl.ds(t * LANES, LANES)
        loads.append(pltpu.make_async_copy(sk_hbm.at[:, across], raw.at[t], load_sem.at[0, t]))
        loads.append(pltpu.make_async_copy(w_hbm.at[:, across], wraw.at[t], load_sem.at[1, t]))
    for load in loads:
        load.start()

    lane = lax.broadcasted_iota(jnp.int32, (SUB, LANES), 1)
    sub = lax.broadcasted_iota(jnp.int32, (SUB, LANES), 0)

    with jax.named_scope("load"):
        for load in loads:
            load.wait()
    def mirror(v):
        return jnp.where(
            sub < 3, pltpu.roll(v, 3, 0), jnp.where(sub < 5, v, pltpu.roll(v, 5, 0))
        )

    def original(r):
        return r + flip * (rows - 1 - 2 * r)

    def relayout(members):
        for r in members:
            r0 = original(r)
            for t in range(tiles):
                for g in range(groups):
                    x[t, r + 2, g * SUB : (g + 1) * SUB, :] = raw[
                        t, pl.ds(g * SUB * rows + r0, SUB, stride=rows), :
                    ]
                v = wraw[t, pl.ds(r0, SUB, stride=rows), :]
                w[t, r + 1] = jnp.where(flip == 1, mirror(v), v)

    outer = [0, 1, rows - 2, rows - 1]
    inner = list(range(2, rows - 2))
    halves = (outer, inner)

    def edge_copy(kind, dc):
        at = 2 * kind + (0 if dc > 0 else 1)
        size = 2 * SUB if kind == SAME else SUB
        return pltpu.make_async_remote_copy(
            src_ref=pack.at[pl.ds(0, size)], dst_ref=nb.at[at, pl.ds(0, size)],
            send_sem=col_send.at[at], recv_sem=col_recv.at[at],
            device_id=at_offset(kind, dc), device_id_type=MESH,
        )

    def row_copies(kind, only=None):
        at = 0 if kind == NEAR else 1
        refs = [(
            w.at[pl.ds(0, tiles), 1 if kind == NEAR else rows],
            w.at[pl.ds(0, tiles), 0 if kind == NEAR else rows + 1],
        )]
        src, dst = (2, 0) if kind == NEAR else (rows, rows + 2)
        for t in range(tiles):
            refs.append((x.at[t, pl.ds(src, 2)], x.at[t, pl.ds(dst, 2)]))
        return [
            pltpu.make_async_remote_copy(
                src_ref=a, dst_ref=b, send_sem=row_send.at[at, k], recv_sem=row_recv.at[at, k],
                device_id=at_offset(kind, 0), device_id_type=MESH,
            )
            for k, (a, b) in enumerate(refs)
            if only is None or k in only
        ]

    with jax.named_scope("relayout"):
        relayout(outer)
    with jax.named_scope("barrier"):
        pl.semaphore_wait(barrier, neighbours)
    with jax.named_scope("rowsends"):
        for kind in (FAR, NEAR):
            @when(kind, 0)
            def _(kind=kind):
                for copy in row_copies(kind):
                    copy.start()
        if rounds > 1:
            greet(reach.at[0])
    with jax.named_scope("relayout2"):
        relayout(inner)
    with jax.named_scope("pack"):
        for h, members in enumerate(halves):
            packed = jnp.zeros((SUB, LANES), f32)
            for at, r in enumerate(members):
                for g in range(groups + 1):
                    if g < groups:
                        slot = at * groups + g
                        first = x[0, r + 2, g * SUB : (g + 1) * SUB, :]
                        final = x[tiles - 1, r + 2, g * SUB : (g + 1) * SUB, :]
                    else:
                        slot = len(members) * groups + at
                        first, final = w[0, r + 1], w[tiles - 1, r + 1]
                    edge = jnp.where(lane < LANES // 2, first, final)
                    moved = pltpu.roll(edge, (4 * slot + 2) % LANES, 1)
                    packed = jnp.where(lane // 4 == slot, moved, packed)
            pack[h * SUB : (h + 1) * SUB, :] = packed
    with jax.named_scope("sends"):
        for kind, dc in around:
            @when(kind, dc)
            def _(kind=kind, dc=dc):
                edge_copy(kind, dc).start()

    @unless(FAR, 0)
    def _():
        for t in range(tiles):
            x[t, rows + 2 : rows + 4] = jnp.zeros((2, n, LANES), f32)
            w[t, rows + 1] = jnp.zeros((SUB, LANES), f32)

    for kind, dc in around:
        @unless(kind, dc)
        def _(kind=kind, dc=dc):
            nb[2 * kind + (1 if dc > 0 else 0)] = jnp.zeros((2 * SUB, LANES), f32)

    edge = tiles
    main = list(range(tiles))
    taken = (lane >= LANES - 2) | ((lane >= 64) & (lane < 66))

    def merge(kind, h):
        at = 2 * kind
        part = pl.ds(h * SUB, SUB)
        return jnp.where(lane % 4 < 2, nb[at, part, :], pltpu.roll(nb[at + 1, part, :], 64, 1))

    def unpack(both, slot):
        return pltpu.roll(both, (-(4 * slot + 2)) % LANES, 1)

    def near(first, final):
        return jnp.where((lane >= 32) & (lane < 96), pltpu.roll(final, 64, 1), first)

    def shift_weights(r, ring):
        size = len(ring)
        taps = [w[t, r + 1] for t in ring]
        ahead = [pltpu.roll(v, LANES - 1, 1) for v in taps]
        behind = [pltpu.roll(v, 1, 1) for v in taps]
        left_taps = (sub == 0) | (sub == 3) | (sub == 5)
        right_taps = (sub == 2) | (sub == 4) | (sub == 7)
        for k, t in enumerate(ring):
            after, before = ahead[k], behind[k]
            if k + 1 < size:
                after = jnp.where(lane == LANES - 1, ahead[k + 1], after)
            if k > 0:
                before = jnp.where(lane == 0, behind[k - 1], before)
            ws[t, r + 1, 0:SUB, :] = jnp.where(
                left_taps, after, jnp.where(right_taps, before, taps[k])
            )
            degree = jnp.sum(taps[k], axis=0, keepdims=True)
            ws[t, r + 1, SUB : 2 * SUB, :] = jnp.broadcast_to(degree, (SUB, LANES))

    def stencil(src, dst, rows_at, ring):
        size = len(ring)
        parts = {}

        def begin(k):
            t = ring[k]
            for at, (near_by, d, r) in enumerate(rows_at):
                tap = [
                    jnp.broadcast_to(ws[t, r + 1, pl.ds(q, 1), :], (SUB, LANES))
                    for q in range(SUB)
                ]
                degree = ws[t, r + 1, SUB : 2 * SUB, :]
                for g in range(groups):
                    part = slice(g * SUB, (g + 1) * SUB)
                    up, here, down = (src[t, e, part, :] for e in near_by)
                    parts[k, at, g] = (
                        degree * here + tap[1] * up + tap[6] * down,
                        pltpu.roll(tap[0] * up + tap[3] * here + tap[5] * down, 1, 1),
                        pltpu.roll(tap[2] * up + tap[4] * here + tap[7] * down, LANES - 1, 1),
                    )

        def end(k):
            for at, (_, d, r) in enumerate(rows_at):
                for g in range(groups):
                    center, low, high = parts[k, at, g]
                    if k > 0:
                        low = jnp.where(lane == 0, parts[k - 1, at, g][1], low)
                    if k + 1 < size:
                        high = jnp.where(lane == LANES - 1, parts[k + 1, at, g][2], high)
                    dst[ring[k], d, g * SUB : (g + 1) * SUB, :] = center + low + high

        return begin, end

    def whole_rows(src, dst, rows_at, ring):
        for row_at in rows_at:
            begin, end = stencil(src, dst, [row_at], ring)
            for k in range(len(ring)):
                begin(k)
                if k > 0:
                    end(k - 1)
            end(len(ring) - 1)

    def x_row(r):
        return {-1: 0, -2: 1, rows: rows + 3, rows + 1: rows + 2}.get(r, r + 2)

    def first_image(members):
        return [((x_row(r - 1), x_row(r), x_row(r + 1)), r + 1, r) for r in members]

    def second_image(members):
        return [((r, r + 1, r + 2), r, r) for r in members]

    def gram(src, picks):
        pieces = []
        for d, with_main, with_edge in picks:
            if with_main:
                for t in main:
                    v = src[t, d]
                    if t == 0:
                        v = jnp.where(wide_lane >= 2, v, 0.0)
                    if t == tiles - 1:
                        v = jnp.where(wide_lane < LANES - 2, v, 0.0)
                    pieces.append(v)
            if with_edge:
                pieces.append(jnp.where(wide_edge, src[edge, d], 0.0))
        both = jnp.concatenate(split(jnp.concatenate(pieces, axis=1)), axis=0)
        return lax.dot_general(both, both, NT, preferred_element_type=f32)

    wide_lane = lax.broadcasted_iota(jnp.int32, (n, LANES), 1)
    wide_edge = (wide_lane < 2) | ((wide_lane >= 62) & (wide_lane < 64))

    with jax.named_scope("weights"):
        for r in range(rows):
            shift_weights(r, main)
    with jax.named_scope("y1in"):
        whole_rows(x, y1, first_image(range(1, rows - 1)), main)
    with jax.named_scope("y2in"):
        whole_rows(y1, y2, second_image(range(2, rows - 2)), main)
    with jax.named_scope("gramin"):
        total_1 = gram(y1, [(r + 1, True, False) for r in range(1, rows - 1)])
        total_2 = gram(y2, [(r, True, False) for r in range(2, rows - 2)])

    if rounds > 1:
        with jax.named_scope("round2"):
            pl.semaphore_wait(reach.at[0], neighbours)
            if rounds > 2:
                greet(reach.at[1])

    def build_edge(kind, members, part_of):
        half, size = part_of
        both = merge(kind, half)
        for r, at in members:
            e = x_row(r)
            for g in range(groups):
                part = slice(g * SUB, (g + 1) * SUB)
                x[edge, e, part, :] = jnp.where(
                    taken, unpack(both, at * groups + g),
                    near(x[0, e, part, :], x[tiles - 1, e, part, :]),
                )
        for r, at in members:
            if -1 <= r <= rows:
                v = unpack(both, size * groups + at)
                if kind != SAME:
                    v = mirror(v)
                w[edge, r + 1] = jnp.where(taken, v, near(w[0, r + 1], w[tiles - 1, r + 1]))

    with jax.named_scope("recvnear"):
        for copy in row_copies(NEAR):
            copy.wait_recv()
    with jax.named_scope("near"):
        for t in main:
            w[t, 0] = mirror(w[t, 0])
        shift_weights(-1, main)
        whole_rows(x, y1, first_image((-1, 0)), main)
        whole_rows(y1, y2, second_image((0, 1)), main)
        total_1 = total_1 + gram(y1, [(1, True, False)])
        total_2 = total_2 + gram(y2, [(r, True, False) for r in (0, 1)])

    with jax.named_scope("recvcols"):
        for kind in (SAME, NEAR):
            for dc in (-1, 1):
                @when(kind, dc)
                def _(kind=kind, dc=dc):
                    edge_copy(kind, -dc).wait_recv()
    with jax.named_scope("edges"):
        for h, members in enumerate(halves):
            build_edge(SAME, [(r, at) for at, r in enumerate(members)], (h, len(members)))
        build_edge(NEAR, [(-1, 0), (-2, 1)], (0, len(outer)))
        for r in range(-1, rows):
            shift_weights(r, [edge])
        whole_rows(x, y1, first_image(range(-1, rows - 1)), [edge])
        whole_rows(y1, y2, second_image(range(rows - 2)), [edge])
        total_1 = total_1 + gram(y1, [(r + 1, False, True) for r in range(rows - 1)])
        total_2 = total_2 + gram(y2, [(r, False, True) for r in range(rows - 2)])

    with jax.named_scope("recvfar1"):
        @when(FAR, 0)
        def _():
            for dc in (-1, 1):
                @when(SAME, dc)
                def _(dc=dc):
                    edge_copy(FAR, -dc).wait_recv()
            row_copies(FAR, (0,))[0].wait_recv()
    with jax.named_scope("far1"):
        for t in main:
            w[t, rows + 1] = mirror(w[t, rows + 1])
        both = merge(FAR, 0)
        v = mirror(unpack(both, len(outer) * groups + 3))
        w[edge, rows + 1] = jnp.where(taken, v, near(w[0, rows + 1], w[tiles - 1, rows + 1]))
        for ring in (main, [edge]):
            shift_weights(rows, ring)
    with jax.named_scope("recvfar2"):
        @when(FAR, 0)
        def _():
            for copy in row_copies(FAR, range(1, tiles + 1)):
                copy.wait_recv()
    with jax.named_scope("far2"):
        for r, at in ((rows, 3), (rows + 1, 2)):
            e = x_row(r)
            for g in range(groups):
                part = slice(g * SUB, (g + 1) * SUB)
                x[edge, e, part, :] = jnp.where(
                    taken, unpack(both, at * groups + g),
                    near(x[0, e, part, :], x[tiles - 1, e, part, :]),
                )
        for ring in (main, [edge]):
            whole_rows(x, y1, first_image((rows - 1, rows)), ring)
        for ring in (main, [edge]):
            whole_rows(y1, y2, second_image((rows - 2, rows - 1)), ring)
        total_1 = total_1 + gram(y1, [(rows, True, True)])
        total_2 = total_2 + gram(y2, [(r, True, True) for r in (rows - 2, rows - 1)])

    scale = 1.0 / (rows * cols * R * C)

    def fold(total):
        half = total[0:n] + total[n : 2 * n]
        square = (half[:, 0:n] + half[:, n : 2 * n]) * scale
        return jnp.concatenate([square[g * SUB : (g + 1) * SUB] for g in range(groups)], axis=1)

    def gather_copies(stage, receiving):
        axes, count = stages[stage]
        me = {"row": i, "col": j, "both": j * R + i}[axes]
        copies = []
        for k in range(count - 1):
            peer = k + (k >= me).astype(jnp.int32)
            slot = peer if receiving else me
            target = {
                "row": {"row": peer, "col": j},
                "col": {"row": i, "col": peer},
                "both": {"row": lax.rem(peer, R), "col": lax.div(peer, R)},
            }[axes]
            copies.append(pltpu.make_async_remote_copy(
                src_ref=sent.at[stage], dst_ref=held.at[stage, slot],
                send_sem=gather_send.at[stage, k],
                recv_sem=gather_recv.at[stage, slot],
                device_id=target, device_id_type=MESH,
            ))
        return copies

    def spread(stage, value, diagonal):
        axes, count = stages[stage]
        me = {"row": i, "col": j, "both": j * R + i}[axes]
        for ref in (sent.at[stage], held.at[stage, me]):
            ref[0:SUB, :] = value
            ref[SUB : SUB + 1, :] = diagonal
        for copy in gather_copies(stage, False):
            copy.start()

    def collect(stage):
        for copy in gather_copies(stage, True):
            copy.wait_recv()
        totals = []
        for part in (slice(0, SUB), slice(SUB, SUB + 1)):
            terms = [held[stage, at, part, :] for at in range(stages[stage][1])]
            while len(terms) > 1:
                terms = [sum(terms[k + 1 : k + 2], terms[k]) for k in range(0, len(terms), 2)]
            totals.append(terms[0])
        return totals

    with jax.named_scope("fold"):
        across, down = lane % n, sub + SUB * (lane // n)
        folded = fold(total_2)
        value = jnp.where(across >= down, fold(total_1), folded)
        diagonal = jnp.sum(jnp.where(across == down, folded, 0.0), axis=0, keepdims=True)
    for k in range(2, rounds):
        with jax.named_scope("round3"):
            pl.semaphore_wait(reach.at[k - 1], neighbours)
            if k + 1 < rounds:
                greet(reach.at[k])
    with jax.named_scope("spread"):
        spread(0, value, diagonal)

    def eliminate(square, diagonal, step=SUB):
        blocks = []
        half = lane % 64
        stacked = jnp.concatenate(
            [square] + [pltpu.roll(square, LANES - g * n, 1) for g in range(1, groups)], axis=0
        )
        turned = stacked.T[0:n]
        diagonal = jnp.broadcast_to(diagonal, (SUB, LANES))
        for g in range(groups):
            part = slice(g * SUB, (g + 1) * SUB)
            row = sub + g * SUB
            mirror = jnp.concatenate([turned[part]] * (LANES // n), axis=1)
            whole = jnp.concatenate([stacked[part, 0:n]] * (LANES // n), axis=1)
            shifted = pltpu.roll(diagonal, (64 - g * n) % LANES, 1)
            first = jnp.where(lane >= row, whole, mirror)
            second = jnp.where(half < row, whole, jnp.where(half == row, shifted, mirror))
            eye = (half - n == row).astype(f32)
            blocks.append(jnp.where(half < n, jnp.where(lane < 64, first, second), eye))

        def over_lanes(v, p):
            return jnp.where(
                lane < 64,
                jnp.broadcast_to(v[:, p : p + 1], (SUB, LANES)),
                jnp.broadcast_to(v[:, 64 + p : 64 + p + 1], (SUB, LANES)),
            )

        solved = [jnp.zeros((SUB, LANES), f32)] * groups
        for p in range(0, n, step):
            home, base = p // SUB, p % SUB
            line = [
                jnp.broadcast_to(blocks[home][base + q : base + q + 1, :], (SUB, LANES))
                for q in range(step)
            ]
            column = {
                (s, g): over_lanes(blocks[g], p + s)
                for g in range(home, groups)
                for s in range(step)
            }
            corner = {
                (q, s): jnp.broadcast_to(column[s, home][base + q : base + q + 1, :], (SUB, LANES))
                for q in range(step)
                for s in range(q, step)
            }
            scaled = []
            for q in range(step):
                over = 1.0 / corner[q, q]
                scaled.append(line[q] * over)
                ratio = {s: corner[q, s] * over for s in range(q + 1, step)}
                for s in range(q + 1, step):
                    line[s] = line[s] - ratio[s] * line[q]
                    for t in range(s, step):
                        corner[s, t] = corner[s, t] - ratio[s] * corner[q, t]
                    for g in range(home + (base + step == SUB), groups):
                        column[s, g] = column[s, g] - ratio[s] * column[q, g]
            for g in range(home + (base + step == SUB), groups):
                update = column[0, g] * scaled[0]
                for q in range(1, step):
                    update = update + column[q, g] * scaled[q]
                blocks[g] = blocks[g] - update
            for q in range(step):
                done = line[q] * lax.rsqrt(corner[q, q])
                solved[home] = jnp.where(sub == base + q, done, solved[home])
        return jnp.concatenate(solved, axis=0)

    for stage in range(1, len(stages)):
        spread(stage, *collect(stage - 1))
    with jax.named_scope("patch"):
        for r in range(rows):
            edges = y2[edge, r]
            pieces = [y2[t, r] for t in main]
            pieces[0] = jnp.where(wide_lane < 2, edges, pieces[0])
            pieces[-1] = jnp.where(wide_lane >= LANES - 2, pltpu.roll(edges, 64, 1), pieces[-1])
            y2_out[original(r)] = jnp.concatenate(split(jnp.concatenate(pieces, axis=1)), axis=0)
    with jax.named_scope("collect"):
        square, diagonal = collect(len(stages) - 1)
    with jax.named_scope("eliminate"):
        tables[...] = eliminate(square, diagonal)

    with jax.named_scope("drain"):
        for kind, dc in around:
            @when(kind, dc)
            def _(kind=kind, dc=dc):
                edge_copy(kind, dc).wait_send()
        for kind in (NEAR, FAR):
            @when(kind, 0)
            def _(kind=kind):
                for copy in row_copies(kind):
                    copy.wait_send()
        for stage in range(len(stages)):
            for copy in gather_copies(stage, False):
                copy.wait_send()


def finish(n, rows, cols, y2, tables, out_ref, fac_ref, staged, fac, store_sem):
    groups = n // SUB
    tiles = cols // LANES
    inv_hi, inv_lo = split(tables[:, 3 * n : 4 * n])
    left = jnp.concatenate([inv_hi, inv_lo, inv_hi], axis=1)
    stores = []
    for t0 in range(0, tiles, 2):
        for r in range(rows):
            hi = y2[r, 0:n, t0 * LANES : (t0 + 2) * LANES]
            lo = y2[r, n : 2 * n, t0 * LANES : (t0 + 2) * LANES]
            right = jnp.concatenate([hi, hi, lo], axis=0)
            solved = jnp.dot(left, right, preferred_element_type=f32)
            for t in range(2):
                for g in range(groups):
                    staged[t0 + t, pl.ds(g * SUB * rows + r, SUB, stride=rows), :] = solved[
                        g * SUB : (g + 1) * SUB, t * LANES : (t + 1) * LANES
                    ]
        for t in range(t0, t0 + 2):
            stores.append(pltpu.make_async_copy(
                staged.at[t], out_ref.at[:, pl.ds(t * LANES, LANES)], store_sem.at[t]
            ))
            stores[-1].start()
    inverse_1 = tables[:, n : 2 * n]
    upper_2 = tables[:, 2 * n : 3 * n]
    row_at = lax.broadcasted_iota(jnp.int32, (n, n), 0)
    col_at = lax.broadcasted_iota(jnp.int32, (n, n), 1)
    upper_2 = jnp.where(col_at >= row_at, upper_2, 0.0)
    last = lax.dot_general(upper_2, inverse_1, NT, precision=HIGHEST, preferred_element_type=f32)
    fac[...] = jnp.where(col_at >= row_at, last, 0.0)
    stores.append(pltpu.make_async_copy(fac, fac_ref, store_sem.at[tiles]))
    stores[-1].start()
    for store in stores:
        store.wait()


def on_device(sketch, weights):
    n, rows, cols = sketch.shape
    R, C = lax.axis_size("row"), lax.axis_size("col")
    tiles = cols // LANES
    stages = (("both", R * C),) if R * C <= 16 else (("row", R), ("col", C))
    rounds = max(R, C) - 1
    peers = max(count for _, count in stages)
    dma = pltpu.SemaphoreType.DMA
    image, tables = pl.pallas_call(
        functools.partial(kernel, n, rows, cols, R, C, stages, rounds),
        out_shape=(
            pltpu.VMEM((rows, 2 * n, cols), bf16),
            pltpu.VMEM((n, LANES), f32),
        ),
        in_specs=[pl.BlockSpec(memory_space=pltpu.HBM)] * 2,
        out_specs=(
            pl.BlockSpec(memory_space=pltpu.VMEM),
            pl.BlockSpec(memory_space=pltpu.VMEM),
        ),
        scratch_shapes=[
            pltpu.VMEM((tiles, n * rows, LANES), f32),
            pltpu.VMEM((tiles, SUB * rows, LANES), f32),
            pltpu.VMEM((tiles + 1, rows + 4, n, LANES), f32),
            pltpu.VMEM((tiles + 1, rows + 2, SUB, LANES), f32),
            pltpu.VMEM((tiles + 1, rows + 2, 2 * SUB, LANES), f32),
            pltpu.VMEM((tiles + 1, rows + 2, n, LANES), f32),
            pltpu.VMEM((tiles + 1, rows, n, LANES), f32),
            pltpu.VMEM((2 * SUB, LANES), f32),
            pltpu.VMEM((6, 2 * SUB, LANES), f32),
            pltpu.VMEM((len(stages), peers, SUB + 1, LANES), f32),
            pltpu.VMEM((len(stages), SUB + 1, LANES), f32),
            dma((2, tiles)), dma((6,)), dma((6,)), dma((2, tiles + 1)), dma((2, tiles + 1)),
            dma((len(stages), peers)), dma((len(stages), peers)),
            pltpu.SemaphoreType.REGULAR((max(rounds - 1, 1),)),
        ],
        compiler_params=pltpu.CompilerParams(
            collective_id=0, has_side_effects=True, vmem_limit_bytes=16 * 1024 * 1024
        ),
    )(
        pltpu.with_memory_space_constraint(sketch.reshape(n * rows, cols), pltpu.HBM),
        pltpu.with_memory_space_constraint(weights.reshape(SUB * rows, cols), pltpu.HBM),
    )
    basis, factor = pl.pallas_call(
        functools.partial(finish, n, rows, cols),
        out_shape=(
            jax.ShapeDtypeStruct((n * rows, cols), f32),
            jax.ShapeDtypeStruct((n, n), f32),
        ),
        in_specs=[pl.BlockSpec(memory_space=pltpu.VMEM)] * 2,
        out_specs=(
            pl.BlockSpec(memory_space=pl.ANY),
            pl.BlockSpec(memory_space=pl.ANY),
        ),
        scratch_shapes=[
            pltpu.VMEM((tiles, n * rows, LANES), f32),
            pltpu.VMEM((n, n), f32),
            dma((tiles + 1,)),
        ],
        compiler_params=pltpu.CompilerParams(vmem_limit_bytes=16 * 1024 * 1024),
    )(image, tables)
    return basis.reshape(n, rows, cols), factor


def solution(mesh):
    return jax.shard_map(
        on_device,
        mesh=mesh,
        in_specs=(P(None, ("sec", "row"), "col"), P(None, ("sec", "row"), "col")),
        out_specs=(P(None, ("sec", "row"), "col"), P("sec", None)),
        check_vma=False,
    )
```

time: 18 us -> 16.9 us (0.939)
  Pallas kernels: 17.2 us -> 16.1 us
    pallas_call x1, Pallas kernels: 16.1 us -> 15 us  [on_device(): pl.pallas_call(functools.partial(kernel, n, rows, cols, R, C, stages, rou...]
where the time goes in v2:
time: 16.9 us; the launch traced here: 16.8 us
  Pallas kernels  16.1 us (95%)
  between operations  0.64 us (4%)
    pallas_call x1, Pallas kernels, on_device(): pl.pallas_call(functools.partial(kernel, n, rows, cols, R, C, stages, rou...  15 us
    pallas_call x1, Pallas kernels, on_device(): pl.pallas_call(functools.partial(finish, n, rows, cols), out_shape=(jax.S...  1.11 us

profile of v2, /device:TPU:0, one launch (start us, length us, event | category | flops | bytes accessed | tf_op | source)
XLA Modules:
  0.0 16.8 jit_solution(6388272495191869118)
XLA Ops:
  0.6 15.0 %shard_map.41 = (bf16[8,64,512]{2,1,0:T(8,128)(2,1)S(1)}, f32[32,128]{1,0:T(8,128)S(1)}) custom-call(f32[256,512]{1,0:T(8,128)} %bitcast.3, f32[64,512]{1,0:T(8,128)} %bitcast.4), custom_call_target="tpu_custom_call" | custom-call | tf_op jit(solution)/shard_map/pallas_call | solution.py:587
  15.7 1.1 %shard_map.42 = (f32[256,512]{1,0:T(8,128)}, f32[32,32]{1,0:T(8,128)}) custom-call(bf16[8,64,512]{2,1,0:T(8,128)(2,1)S(1)} %get-tuple-element.6.y2, f32[32,128]{1,0:T(8,128)S(1)} %get-tuple-element.7.tables), custom_call_target="tpu_custom_call" | custom-call | tf_op jit(solution)/shard_map/pallas_call | solution.py:621

commit v3 on v2

--- a/solution.py
+++ b/solution.py
@@ -137,19 +137,7 @@
         ]
 
     with jax.named_scope("relayout"):
-        relayout(outer)
-    with jax.named_scope("barrier"):
-        pl.semaphore_wait(barrier, neighbours)
-    with jax.named_scope("rowsends"):
-        for kind in (FAR, NEAR):
-            @when(kind, 0)
-            def _(kind=kind):
-                for copy in row_copies(kind):
-                    copy.start()
-        if rounds > 1:
-            greet(reach.at[0])
-    with jax.named_scope("relayout2"):
-        relayout(inner)
+        relayout(range(rows))
     with jax.named_scope("pack"):
         for h, members in enumerate(halves):
             packed = jnp.zeros((SUB, LANES), f32)
@@ -166,11 +154,21 @@
                     moved = pltpu.roll(edge, (4 * slot + 2) % LANES, 1)
                     packed = jnp.where(lane // 4 == slot, moved, packed)
             pack[h * SUB : (h + 1) * SUB, :] = packed
+    with jax.named_scope("barrier"):
+        pl.semaphore_wait(barrier, neighbours)
     with jax.named_scope("sends"):
         for kind, dc in around:
             @when(kind, dc)
             def _(kind=kind, dc=dc):
                 edge_copy(kind, dc).start()
+    with jax.named_scope("rowsends"):
+        for kind in (FAR, NEAR):
+            @when(kind, 0)
+            def _(kind=kind):
+                for copy in row_copies(kind):
+                    copy.start()
+        if rounds > 1:
+            greet(reach.at[0])
 
     @unless(FAR, 0)
     def _():
@@ -335,31 +333,21 @@
         total_2 = total_2 + gram(y2, [(r, True, False) for r in (0, 1)])
 
     with jax.named_scope("recvcols"):
-        for kind in (SAME, NEAR):
+        for kind in (SAME, NEAR, FAR):
             for dc in (-1, 1):
                 @when(kind, dc)
                 def _(kind=kind, dc=dc):
                     edge_copy(kind, -dc).wait_recv()
+
+        @when(FAR, 0)
+        def _():
+            row_copies(FAR, (0,))[0].wait_recv()
     with jax.named_scope("edges"):
         for h, members in enumerate(halves):
             build_edge(SAME, [(r, at) for at, r in enumerate(members)], (h, len(members)))
         build_edge(NEAR, [(-1, 0), (-2, 1)], (0, len(outer)))
         for r in range(-1, rows):
             shift_weights(r, [edge])
-        whole_rows(x, y1, first_image(range(-1, rows - 1)), [edge])
-        whole_rows(y1, y2, second_image(range(rows - 2)), [edge])
-        total_1 = total_1 + gram(y1, [(r + 1, False, True) for r in range(rows - 1)])
-        total_2 = total_2 + gram(y2, [(r, False, True) for r in range(rows - 2)])
-
-    with jax.named_scope("recvfar1"):
-        @when(FAR, 0)
-        def _():
-            for dc in (-1, 1):
-                @when(SAME, dc)
-                def _(dc=dc):
-                    edge_copy(FAR, -dc).wait_recv()
-            row_copies(FAR, (0,))[0].wait_recv()
-    with jax.named_scope("far1"):
         for t in main:
             w[t, rows + 1] = mirror(w[t, rows + 1])
         both = merge(FAR, 0)
@@ -367,6 +355,11 @@
         w[edge, rows + 1] = jnp.where(taken, v, near(w[0, rows + 1], w[tiles - 1, rows + 1]))
         for ring in (main, [edge]):
             shift_weights(rows, ring)
+        whole_rows(x, y1, first_image(range(-1, rows - 1)), [edge])
+        whole_rows(y1, y2, second_image(range(rows - 2)), [edge])
+        total_1 = total_1 + gram(y1, [(r + 1, False, True) for r in range(rows - 1)])
+        total_2 = total_2 + gram(y2, [(r, False, True) for r in range(rows - 2)])
+
     with jax.named_scope("recvfar2"):
         @when(FAR, 0)
         def _():
@@ -572,8 +565,9 @@
     fac[...] = jnp.where(col_at >= row_at, last, 0.0)
     stores.append(pltpu.make_async_copy(fac, fac_ref, store_sem.at[tiles]))
     stores[-1].start()
-    for store in stores:
-        store.wait()
+    with jax.named_scope("storewait"):
+        for store in stores:
+            store.wait()
 
 
 def on_device(sketch, weights):

time: 16.9 us -> 16.6 us (0.982)
  Pallas kernels: 16.1 us -> 15.8 us
    pallas_call x1, Pallas kernels: 15 us -> 14.7 us  [on_device(): pl.pallas_call(functools.partial(kernel, n, rows, cols, R, C, stages, rou...]
where the time goes in v3:
time: 16.6 us; the launch traced here: 16.5 us
  Pallas kernels  15.8 us (95%)
  between operations  0.64 us (4%)
    pallas_call x1, Pallas kernels, on_device(): pl.pallas_call(functools.partial(kernel, n, rows, cols, R, C, stages, rou...  14.7 us
    pallas_call x1, Pallas kernels, on_device(): pl.pallas_call(functools.partial(finish, n, rows, cols), out_shape=(jax.S...  1.11 us

profile of v3, /device:TPU:0, one launch (start us, length us, event | category | flops | bytes accessed | tf_op | source)
XLA Modules:
  0.0 16.5 jit_solution(18088402660236871648)
XLA Ops:
  0.6 14.7 %shard_map.41 = (bf16[8,64,512]{2,1,0:T(8,128)(2,1)S(1)}, f32[32,128]{1,0:T(8,128)S(1)}) custom-call(f32[256,512]{1,0:T(8,128)} %bitcast.3, f32[64,512]{1,0:T(8,128)} %bitcast.4), custom_call_target="tpu_custom_call" | custom-call | tf_op jit(solution)/shard_map/pallas_call | solution.py:581
  15.4 1.1 %shard_map.42 = (f32[256,512]{1,0:T(8,128)}, f32[32,32]{1,0:T(8,128)}) custom-call(bf16[8,64,512]{2,1,0:T(8,128)(2,1)S(1)} %get-tuple-element.6.y2, f32[32,128]{1,0:T(8,128)S(1)} %get-tuple-element.7.tables), custom_call_target="tpu_custom_call" | custom-call | tf_op jit(solution)/shard_map/pallas_call | solution.py:615

commit v4 on v3

--- a/solution.py
+++ b/solution.py
@@ -83,9 +83,8 @@
     lane = lax.broadcasted_iota(jnp.int32, (SUB, LANES), 1)
     sub = lax.broadcasted_iota(jnp.int32, (SUB, LANES), 0)
 
-    with jax.named_scope("load"):
-        for load in loads:
-            load.wait()
+    for load in loads:
+        load.wait()
     def mirror(v):
         return jnp.where(
             sub < 3, pltpu.roll(v, 3, 0), jnp.where(sub < 5, v, pltpu.roll(v, 5, 0))
@@ -136,39 +135,34 @@
             if only is None or k in only
         ]
 
-    with jax.named_scope("relayout"):
-        relayout(range(rows))
-    with jax.named_scope("pack"):
-        for h, members in enumerate(halves):
-            packed = jnp.zeros((SUB, LANES), f32)
-            for at, r in enumerate(members):
-                for g in range(groups + 1):
-                    if g < groups:
-                        slot = at * groups + g
-                        first = x[0, r + 2, g * SUB : (g + 1) * SUB, :]
-                        final = x[tiles - 1, r + 2, g * SUB : (g + 1) * SUB, :]
-                    else:
-                        slot = len(members) * groups + at
-                        first, final = w[0, r + 1], w[tiles - 1, r + 1]
-                    edge = jnp.where(lane < LANES // 2, first, final)
-                    moved = pltpu.roll(edge, (4 * slot + 2) % LANES, 1)
-                    packed = jnp.where(lane // 4 == slot, moved, packed)
-            pack[h * SUB : (h + 1) * SUB, :] = packed
-    with jax.named_scope("barrier"):
-        pl.semaphore_wait(barrier, neighbours)
-    with jax.named_scope("sends"):
-        for kind, dc in around:
-            @when(kind, dc)
-            def _(kind=kind, dc=dc):
-                edge_copy(kind, dc).start()
-    with jax.named_scope("rowsends"):
-        for kind in (FAR, NEAR):
-            @when(kind, 0)
-            def _(kind=kind):
-                for copy in row_copies(kind):
-                    copy.start()
-        if rounds > 1:
-            greet(reach.at[0])
+    relayout(range(rows))
+    for h, members in enumerate(halves):
+        packed = jnp.zeros((SUB, LANES), f32)
+        for at, r in enumerate(members):
+            for g in range(groups + 1):
+                if g < groups:
+                    slot = at * groups + g
+                    first = x[0, r + 2, g * SUB : (g + 1) * SUB, :]
+                    final = x[tiles - 1, r + 2, g * SUB : (g + 1) * SUB, :]
+                else:
+                    slot = len(members) * groups + at
+                    first, final = w[0, r + 1], w[tiles - 1, r + 1]
+                edge = jnp.where(lane < LANES // 2, first, final)
+                moved = pltpu.roll(edge, (4 * slot + 2) % LANES, 1)
+                packed = jnp.where(lane // 4 == slot, moved, packed)
+        pack[h * SUB : (h + 1) * SUB, :] = packed
+    pl.semaphore_wait(barrier, neighbours)
+    for kind, dc in around:
+        @when(kind, dc)
+        def _(kind=kind, dc=dc):
+            edge_copy(kind, dc).start()
+    for kind in (FAR, NEAR):
+        @when(kind, 0)
+        def _(kind=kind):
+            for copy in row_copies(kind):
+                copy.start()
+    if rounds > 1:
+        greet(reach.at[0])
 
     @unless(FAR, 0)
     def _():
@@ -285,22 +279,17 @@
     wide_lane = lax.broadcasted_iota(jnp.int32, (n, LANES), 1)
     wide_edge = (wide_lane < 2) | ((wide_lane >= 62) & (wide_lane < 64))
 
-    with jax.named_scope("weights"):
-        for r in range(rows):
-            shift_weights(r, main)
-    with jax.named_scope("y1in"):
-        whole_rows(x, y1, first_image(range(1, rows - 1)), main)
-    with jax.named_scope("y2in"):
-        whole_rows(y1, y2, second_image(range(2, rows - 2)), main)
-    with jax.named_scope("gramin"):
-        total_1 = gram(y1, [(r + 1, True, False) for r in range(1, rows - 1)])
-        total_2 = gram(y2, [(r, True, False) for r in range(2, rows - 2)])
+    for r in range(rows):
+        shift_weights(r, main)
+    whole_rows(x, y1, first_image(range(1, rows - 1)), main)
+    whole_rows(y1, y2, second_image(range(2, rows - 2)), main)
+    total_1 = gram(y1, [(r + 1, True, False) for r in range(1, rows - 1)])
+    total_2 = gram(y2, [(r, True, False) for r in range(2, rows - 2)])
 
     if rounds > 1:
-        with jax.named_scope("round2"):
-            pl.semaphore_wait(reach.at[0], neighbours)
-            if rounds > 2:
-                greet(reach.at[1])
+        pl.semaphore_wait(reach.at[0], neighbours)
+        if rounds > 2:
+            greet(reach.at[1])
 
     def build_edge(kind, members, part_of):
         half, size = part_of
@@ -320,66 +309,60 @@
                     v = mirror(v)
                 w[edge, r + 1] = jnp.where(taken, v, near(w[0, r + 1], w[tiles - 1, r + 1]))
 
-    with jax.named_scope("recvnear"):
-        for copy in row_copies(NEAR):
+    for copy in row_copies(NEAR):
+        copy.wait_recv()
+    for t in main:
+        w[t, 0] = mirror(w[t, 0])
+    shift_weights(-1, main)
+    whole_rows(x, y1, first_image((-1, 0)), main)
+    whole_rows(y1, y2, second_image((0, 1)), main)
+    total_1 = total_1 + gram(y1, [(1, True, False)])
+    total_2 = total_2 + gram(y2, [(r, True, False) for r in (0, 1)])
+
+    for kind in (SAME, NEAR, FAR):
+        for dc in (-1, 1):
+            @when(kind, dc)
+            def _(kind=kind, dc=dc):
+                edge_copy(kind, -dc).wait_recv()
+
+    @when(FAR, 0)
+    def _():
+        row_copies(FAR, (0,))[0].wait_recv()
+    for h, members in enumerate(halves):
+        build_edge(SAME, [(r, at) for at, r in enumerate(members)], (h, len(members)))
+    build_edge(NEAR, [(-1, 0), (-2, 1)], (0, len(outer)))
+    for r in range(-1, rows):
+        shift_weights(r, [edge])
+    for t in main:
+        w[t, rows + 1] = mirror(w[t, rows + 1])
+    both = merge(FAR, 0)
+    v = mirror(unpack(both, len(outer) * groups + 3))
+    w[edge, rows + 1] = jnp.where(taken, v, near(w[0, rows + 1], w[tiles - 1, rows + 1]))
+    for ring in (main, [edge]):
+        shift_weights(rows, ring)
+    whole_rows(x, y1, first_image(range(-1, rows - 1)), [edge])
+    whole_rows(y1, y2, second_image(range(rows - 2)), [edge])
+    total_1 = total_1 + gram(y1, [(r + 1, False, True) for r in range(rows - 1)])
+    total_2 = total_2 + gram(y2, [(r, False, True) for r in range(rows - 2)])
+
+    @when(FAR, 0)
+    def _():
+        for copy in row_copies(FAR, range(1, tiles + 1)):
             copy.wait_recv()
-    with jax.named_scope("near"):
-        for t in main:
-            w[t, 0] = mirror(w[t, 0])
-        shift_weights(-1, main)
-        whole_rows(x, y1, first_image((-1, 0)), main)
-        whole_rows(y1, y2, second_image((0, 1)), main)
-        total_1 = total_1 + gram(y1, [(1, True, False)])
-        total_2 = total_2 + gram(y2, [(r, True, False) for r in (0, 1)])
-
-    with jax.named_scope("recvcols"):
-        for kind in (SAME, NEAR, FAR):
-            for dc in (-1, 1):
-                @when(kind, dc)
-                def _(kind=kind, dc=dc):
-                    edge_copy(kind, -dc).wait_recv()
-
-        @when(FAR, 0)
-        def _():
-            row_copies(FAR, (0,))[0].wait_recv()
-    with jax.named_scope("edges"):
-        for h, members in enumerate(halves):
-            build_edge(SAME, [(r, at) for at, r in enumerate(members)], (h, len(members)))
-        build_edge(NEAR, [(-1, 0), (-2, 1)], (0, len(outer)))
-        for r in range(-1, rows):
-            shift_weights(r, [edge])
-        for t in main:
-            w[t, rows + 1] = mirror(w[t, rows + 1])
-        both = merge(FAR, 0)
-        v = mirror(unpack(both, len(outer) * groups + 3))
-        w[edge, rows + 1] = jnp.where(taken, v, near(w[0, rows + 1], w[tiles - 1, rows + 1]))
-        for ring in (main, [edge]):
-            shift_weights(rows, ring)
-        whole_rows(x, y1, first_image(range(-1, rows - 1)), [edge])
-        whole_rows(y1, y2, second_image(range(rows - 2)), [edge])
-        total_1 = total_1 + gram(y1, [(r + 1, False, True) for r in range(rows - 1)])
-        total_2 = total_2 + gram(y2, [(r, False, True) for r in range(rows - 2)])
-
-    with jax.named_scope("recvfar2"):
-        @when(FAR, 0)
-        def _():
-            for copy in row_copies(FAR, range(1, tiles + 1)):
-                copy.wait_recv()
-    with jax.named_scope("far2"):
-        for r, at in ((rows, 3), (rows + 1, 2)):
-            e = x_row(r)
-            for g in range(groups):
-                part = slice(g * SUB, (g + 1) * SUB)
-                x[edge, e, part, :] = jnp.where(
-                    taken, unpack(both, at * groups + g),
-                    near(x[0, e, part, :], x[tiles - 1, e, part, :]),
-                )
-        for ring in (main, [edge]):
-            whole_rows(x, y1, first_image((rows - 1, rows)), ring)
-        for ring in (main, [edge]):
-            whole_rows(y1, y2, second_image((rows - 2, rows - 1)), ring)
-        total_1 = total_1 + gram(y1, [(rows, True, True)])
-        total_2 = total_2 + gram(y2, [(r, True, True) for r in (rows - 2, rows - 1)])
+    for r, at in ((rows, 3), (rows + 1, 2)):
+        e = x_row(r)
+        for g in range(groups):
+            part = slice(g * SUB, (g + 1) * SUB)
+            x[edge, e, part, :] = jnp.where(
+                taken, unpack(both, at * groups + g),
+                near(x[0, e, part, :], x[tiles - 1, e, part, :]),
+            )
+    for ring in (main, [edge]):
+        whole_rows(x, y1, first_image((rows - 1, rows)), ring)
+    total_1 = total_1 + gram(y1, [(rows, True, True)])
+    for ring in (main, [edge]):
+        whole_rows(y1, y2, second_image((rows - 2, rows - 1)), ring)
+    total_2 = total_2 + gram(y2, [(r, True, True) for r in (rows - 2, rows - 1)])
 
     scale = 1.0 / (rows * cols * R * C)
 
@@ -428,18 +411,15 @@
             totals.append(terms[0])
         return totals
 
-    with jax.named_scope("fold"):
-        across, down = lane % n, sub + SUB * (lane // n)
-        folded = fold(total_2)
-        value = jnp.where(across >= down, fold(total_1), folded)
-        diagonal = jnp.sum(jnp.where(across == down, folded, 0.0), axis=0, keepdims=True)
+    across, down = lane % n, sub + SUB * (lane // n)
+    folded = fold(total_2)
+    value = jnp.where(across >= down, fold(total_1), folded)
+    diagonal = jnp.sum(jnp.where(across == down, folded, 0.0), axis=0, keepdims=True)
     for k in range(2, rounds):
-        with jax.named_scope("round3"):
-            pl.semaphore_wait(reach.at[k - 1], neighbours)
-            if k + 1 < rounds:
-                greet(reach.at[k])
-    with jax.named_scope("spread"):
-        spread(0, value, diagonal)
+        pl.semaphore_wait(reach.at[k - 1], neighbours)
+        if k + 1 < rounds:
+            greet(reach.at[k])
+    spread(0, value, diagonal)
 
     def eliminate(square, diagonal, step=SUB):
         blocks = []
@@ -507,31 +487,28 @@
 
     for stage in range(1, len(stages)):
         spread(stage, *collect(stage - 1))
-    with jax.named_scope("patch"):
-        for r in range(rows):
-            edges = y2[edge, r]
-            pieces = [y2[t, r] for t in main]
-            pieces[0] = jnp.where(wide_lane < 2, edges, pieces[0])
-            pieces[-1] = jnp.where(wide_lane >= LANES - 2, pltpu.roll(edges, 64, 1), pieces[-1])
-            y2_out[original(r)] = jnp.concatenate(split(jnp.concatenate(pieces, axis=1)), axis=0)
-    with jax.named_scope("collect"):
-        square, diagonal = collect(len(stages) - 1)
-    with jax.named_scope("eliminate"):
-        tables[...] = eliminate(square, diagonal)
-
-    with jax.named_scope("drain"):
-        for kind, dc in around:
-            @when(kind, dc)
-            def _(kind=kind, dc=dc):
-                edge_copy(kind, dc).wait_send()
-        for kind in (NEAR, FAR):
-            @when(kind, 0)
-            def _(kind=kind):
-                for copy in row_copies(kind):
-                    copy.wait_send()
-        for stage in range(len(stages)):
-            for copy in gather_copies(stage, False):
+    for r in range(rows):
+        edges = y2[edge, r]
+        pieces = [y2[t, r] for t in main]
+        pieces[0] = jnp.where(wide_lane < 2, edges, pieces[0])
+        pieces[-1] = jnp.where(wide_lane >= LANES - 2, pltpu.roll(edges, 64, 1), pieces[-1])
+        y2_out[original(r)] = jnp.concatenate(split(jnp.concatenate(pieces, axis=1)), axis=0)
+    for kind, dc in around:
+        @when(kind, dc)
+        def _(kind=kind, dc=dc):
+            edge_copy(kind, dc).wait_send()
+    for kind in (NEAR, FAR):
+        @when(kind, 0)
+        def _(kind=kind):
+            for copy in row_copies(kind):
                 copy.wait_send()
+
+    square, diagonal = collect(len(stages) - 1)
+    tables[...] = eliminate(square, diagonal)
+
+    for stage in range(len(stages)):
+        for copy in gather_copies(stage, False):
+            copy.wait_send()
 
 
 def finish(n, rows, cols, y2, tables, out_ref, fac_ref, staged, fac, store_sem):
@@ -565,9 +542,8 @@
     fac[...] = jnp.where(col_at >= row_at, last, 0.0)
     stores.append(pltpu.make_async_copy(fac, fac_ref, store_sem.at[tiles]))
     stores[-1].start()
-    with jax.named_scope("storewait"):
-        for store in stores:
-            store.wait()
+    for store in stores:
+        store.wait()
 
 
 def on_device(sketch, weights):

time: 16.6 us -> 16.6 us (level)
  no operation moved by 1% of the time
where the time goes in v4:
time: 16.6 us; the launch traced here: 16.5 us
  Pallas kernels  15.8 us (95%)
  between operations  0.64 us (4%)
    pallas_call x1, Pallas kernels, on_device(): pl.pallas_call(functools.partial(kernel, n, rows, cols, R, C, stages, rou...  14.7 us
    pallas_call x1, Pallas kernels, on_device(): pl.pallas_call(functools.partial(finish, n, rows, cols), out_shape=(jax.S...  1.11 us

profile of v4, /device:TPU:0, one launch (start us, length us, event | category | flops | bytes accessed | tf_op | source)
XLA Modules:
  0.0 16.5 jit_solution(9623372410564922246)
XLA Ops:
  0.6 14.7 %shard_map.41 = (bf16[8,64,512]{2,1,0:T(8,128)(2,1)S(1)}, f32[32,128]{1,0:T(8,128)S(1)}) custom-call(f32[256,512]{1,0:T(8,128)} %bitcast.3, f32[64,512]{1,0:T(8,128)} %bitcast.4), custom_call_target="tpu_custom_call" | custom-call | tf_op jit(solution)/shard_map/pallas_call | solution.py:557
  15.4 1.1 %shard_map.42 = (f32[256,512]{1,0:T(8,128)}, f32[32,32]{1,0:T(8,128)}) custom-call(bf16[8,64,512]{2,1,0:T(8,128)(2,1)S(1)} %get-tuple-element.6.y2, f32[32,128]{1,0:T(8,128)S(1)} %get-tuple-element.7.tables), custom_call_target="tpu_custom_call" | custom-call | tf_op jit(solution)/shard_map/pallas_call | solution.py:591
